TPU v7x, 32 devices: a whole 2x2x4 slice. The times are simulated.
32 devices in a mesh: ifg: 8 (over z, x), grp: 4 (over y, core).
Axes of the slice: x: 2, y: 2, z: 4, core: 2. Of those that a mesh axis runs over, the one named last changes fastest.
Arguments:
- phases: bfloat16 [1024, 4, 32768], P('ifg', 'grp'), may hold values from -6 to 6
- date_pairs: int32 [2, 1024], replicated, may hold values from 0 to 199, as said below
- pair_counts: int32 [16], replicated, may hold values from 128 to 1024, as said below
- group_ids: int32 [4, 128], P(None, 'ifg'), may hold values from 0 to 15, as said below
Outputs:
- series: float32 [4, 200, 32768], P('grp', None, 'ifg')
Inputs may be any that keep to these rules, and one draw needn't show every extreme that they name: date_pairs[0, k] < date_pairs[1, k]; the baseline date_pairs[1, k] - date_pairs[0, k] lies in 1 to 25 and never falls as k grows. `pair_counts`: each count is 128 times a power of two; some class has all 1024 interferograms and some has 128. `group_ids`: constant over each aligned run of 8 blocks of a sub-strip.
All inputs are finite; a program needn't handle non-finite values.
Results may differ from a plain program's by a relative error of at most 0.0003.
Values may be sent and summed in bfloat16 or wider, within the bound.
No kernel may reach another device: no remote copies, remote signals or barrier semaphores. Data moves between devices by JAX's collectives and lax.ppermute only.
A program may use at most 128 MiB of HBM per device.

v0:
```python
import functools

import jax
import jax.numpy as jnp
import numpy as np
from jax import lax
from jax.experimental import pallas as pl
from jax.experimental.pallas import tpu as pltpu
from jax.sharding import PartitionSpec as P

M = 200
RUN = 8
PAD = 256
SLABS = 8
DAMPING = 1.0
VMEM_BYTES = 48 * 1024 * 1024
F32 = jnp.float32
HIGHEST = lax.Precision.HIGHEST
STEADY = pl.CostEstimate(flops=10_000_000_000, bytes_accessed=30_000_000, transcendentals=0)
LITTLE = pl.CostEstimate(flops=1024, bytes_accessed=1024, transcendentals=0)
CUTS = 2
HALVES = 2
FLIGHT = 2
FIRST_SWAPS = ((0, 1), (1, 1), (2, 2))
SWAPS = {2: (4, 2), 3: (6, 2), 5: (8, 2), 6: (10, 2), 7: (12, 4)}
SWAP_WAITS = {5: 7, 7: 9, 8: 11, 10: 12}
MEETINGS = (1, 3, 5, 7, 8, 10)
INVERSE_STEP = 2
ME, PARTNER, INNER, FIXED = 0, 1, 2, 3
LATE = 2
LANES = 128
CODE_ROWS = 16
LEVELS = 32700.0
ROUNDER = 1.5 * 2.0**23
CODES_PER_OCTAVE = 128.0
SMALLEST = 2.0**-110
CHUNK_ORDER = ((3, 2, 1, 0), (0, 3, 2, 1), (3, 0, 1, 2), (0, 1, 2, 3))
SENDS = (
    (((0, 1), (1, 0), (2, 3), (3, 2)),),
    (((0, 1), (1, 3), (2, 0), (3, 2)),),
    (((0, 1), (3, 2)), ((1, 2), (2, 1))),
)


def incidence(earlier, later, rows):
    shape = (rows, earlier.shape[1])
    date = lax.broadcasted_iota(jnp.int32, shape, 0)
    return (date == later).astype(F32) - (date == earlier).astype(F32)


def split_product(left, right):
    def halves(value):
        high = value.astype(jnp.bfloat16)
        return high, (value - high.astype(F32)).astype(jnp.bfloat16)

    left_high, left_low = halves(left)
    right_high, right_low = halves(right)
    small = jnp.dot(left_high, right_low, preferred_element_type=F32) + jnp.dot(left_low, right_high, preferred_element_type=F32)
    return jnp.dot(left_high, right_high, preferred_element_type=F32) + small


def full_product(left, right):
    return jnp.dot(left, right, precision=HIGHEST, preferred_element_type=F32)


def inverse_kernel(counts_ref, pairs_ref, *rest):
    out_ref = rest[-1]
    runs = out_ref.shape[0]
    design = incidence(pairs_ref[0:1, :], pairs_ref[1:2, :], PAD)
    pair = lax.broadcasted_iota(jnp.int32, design.shape, 1)
    contract_last = (((1,), (1,)), ((), ()))
    row = lax.broadcasted_iota(jnp.int32, (PAD, PAD), 0)
    col = lax.broadcasted_iota(jnp.int32, (PAD, PAD), 1)
    identity = (row == col).astype(F32)
    grams = []
    for run in range(runs):
        kept = jnp.where(pair < counts_ref[run], design, 0.0).astype(jnp.bfloat16)
        gram = lax.dot_general(kept, kept, contract_last, preferred_element_type=F32)
        grams.append(gram + DAMPING * identity)
    low = DAMPING
    high = 2.0 * functools.reduce(jnp.maximum, [jnp.max(gram) for gram in grams]) - DAMPING
    total, width = high + low, high - low
    scale = 2.0 * total * total - width * width
    starts = tuple((8.0 * total / scale) * identity - (8.0 / scale) * gram for gram in grams)
    needed = 18.0 * scale / (8.0 * high * low)
    steps = jnp.int32(0)
    for power in range(1, 16):
        steps += (needed > float(2**power)).astype(jnp.int32)

    def newton(product, guesses):
        products = [product(gram, guess) for gram, guess in zip(grams, guesses)]
        return tuple(2.0 * guess - product(guess, each) for guess, each in zip(guesses, products))

    full_steps = 1 + (high > 100.0).astype(jnp.int32)
    guesses = lax.fori_loop(0, steps + 1 - full_steps, lambda _, guesses: newton(split_product, guesses), starts)
    guesses = lax.fori_loop(0, full_steps, lambda _, guesses: newton(full_product, guesses), guesses)
    for run, guess in enumerate(guesses):
        out_ref[run] = guess


def invert_classes(date_pairs, run_counts, after):
    shape = (run_counts.shape[0], PAD, PAD)
    return pl.pallas_call(
        inverse_kernel,
        out_shape=jax.ShapeDtypeStruct(shape, F32),
        grid_spec=pltpu.PrefetchScalarGridSpec(
            num_scalar_prefetch=1,
            grid=(1,),
            in_specs=[pl.BlockSpec(date_pairs.shape, lambda i, c: (0, 0))] + [pl.BlockSpec(memory_space=pl.ANY)] * len(after),
            out_specs=pl.BlockSpec(shape, lambda i, c: (0, 0, 0)),
        ),
        compiler_params=pltpu.CompilerParams(vmem_limit_bytes=VMEM_BYTES),
        cost_estimate=LITTLE,
        name="invert_classes_0",
    )(run_counts, date_pairs, *after)


def sum_solve_kernel(tiles, counts_ref, pairs_ref, data_ref, inverse_ref, out_ref):
    run = pl.program_id(0) // tiles
    design = incidence(pairs_ref[0:1, :], pairs_ref[1:2, :], PAD)
    pair = lax.broadcasted_iota(jnp.int32, design.shape, 1)
    kept = jnp.where(pair < counts_ref[run], design, 0.0).astype(jnp.bfloat16)
    sums = jnp.dot(kept, data_ref[...], preferred_element_type=F32)
    out_ref[...] = jnp.dot(inverse_ref[0, :M, :], sums, precision=HIGHEST, preferred_element_type=F32)


def sum_solve(run_counts, date_pairs, received, inverse):
    runs = run_counts.shape[0]
    total_pairs, pixels = received.shape
    run_pixels = pixels // runs
    tile = run_pixels // 2
    tiles = run_pixels // tile
    return pl.pallas_call(
        functools.partial(sum_solve_kernel, tiles),
        out_shape=jax.ShapeDtypeStruct((M, pixels), F32),
        grid_spec=pltpu.PrefetchScalarGridSpec(
            num_scalar_prefetch=1,
            grid=(runs * tiles,),
            in_specs=[
                pl.BlockSpec(date_pairs.shape, lambda i, c: (0, 0)),
                pl.BlockSpec((total_pairs, tile), lambda i, c: (0, i)),
                pl.BlockSpec((1, PAD, PAD), lambda i, c: (i // tiles, 0, 0)),
            ],
            out_specs=pl.BlockSpec((M, tile), lambda i, c: (0, i)),
        ),
        compiler_params=pltpu.CompilerParams(vmem_limit_bytes=VMEM_BYTES),
        name="sum_solve",
    )(run_counts, date_pairs, received, inverse)


def coded_rows(piece):
    return M * (piece // LANES) + CODE_ROWS


def decode(coded_ref, codes_ref, lots, first):
    coded = coded_ref[...].astype(jnp.int32).astype(F32)
    values = jnp.concatenate([coded[lot * M : (lot + 1) * M, :] for lot in range(lots)], axis=1)
    codes = codes_ref[...].astype(jnp.int32).astype(F32)
    codes = jnp.concatenate([codes[first + lot : first + lot + 1, :] for lot in range(lots)], axis=1)
    return values, jnp.exp2(codes * (1.0 / CODES_PER_OCTAVE)) * (1.0 / LEVELS)


def encode(sums):
    largest = jnp.max(jnp.abs(sums), axis=0, keepdims=True)
    code = jnp.ceil(jnp.log2(jnp.maximum(largest, SMALLEST)) * CODES_PER_OCTAVE)
    scaled = (sums * (LEVELS / jnp.exp2(code * (1.0 / CODES_PER_OCTAVE))) + ROUNDER) - ROUNDER
    lots = sums.shape[1] // LANES
    return jnp.concatenate([scaled[:, lot * LANES : (lot + 1) * LANES] for lot in range(lots)], axis=0), code


def whole(values):
    return values.astype(jnp.int32).astype(jnp.int16)


def piece_count(at, layout, table, counts):
    parts, _, _, shifts = layout
    run = at % parts // CUTS
    return counts[table[shifts + at] * (parts // CUTS) + run]


def pair_sums(count, table, pairs_ref, own_ref, partner_ref):
    width = own_ref.shape[0]
    lane = lax.broadcasted_iota(jnp.int32, (1, 2 * width), 1)
    pair = jnp.where(lane < width, table[ME] * width + lane, table[PARTNER] * width + lane - width)
    design = incidence(pairs_ref[0:1, :], pairs_ref[1:2, :], M)
    kept = jnp.where(pair < count, design, 0.0).astype(jnp.bfloat16)
    data = jnp.concatenate([own_ref[...], partner_ref[...]], axis=0)
    return jnp.dot(kept, data, preferred_element_type=F32)


def copy_kernel(table, source_ref, _, target_ref):
    target_ref[...] = source_ref[...]


def give_out(swap, layout, table, phases, after, piece):
    first, count = swap
    away = layout[2]
    shape = (phases.shape[0], piece * count)
    return pl.pallas_call(
        copy_kernel,
        out_shape=jax.ShapeDtypeStruct(shape, phases.dtype),
        grid_spec=pltpu.PrefetchScalarGridSpec(
            num_scalar_prefetch=1,
            grid=(1,),
            in_specs=[
                pl.BlockSpec(shape, lambda i, t: (0, t[away + first] // count)),
                pl.BlockSpec(memory_space=pl.ANY),
            ],
            out_specs=pl.BlockSpec(shape, lambda i, t: (0, 0)),
        ),
        compiler_params=pltpu.CompilerParams(vmem_limit_bytes=VMEM_BYTES),
        cost_estimate=LITTLE,
        name="give_out",
    )(table, phases, after)


def step_kernel(at, layout, adds, swaps, tells, halves, table, counts, pairs_ref, own_ref, partner_ref, *rest):
    if tells:
        rest[-1][...] = jnp.zeros_like(rest[-1])
        rest = rest[:-1]
    if swaps:
        rest[-1][...] = rest[0][...]
        coded_ref, rest = rest[-2], rest[1:]
    else:
        coded_ref = rest[-1]
    count = piece_count(at, layout, table, counts)
    width = own_ref.shape[1] // halves
    lots = width // LANES
    codes = []
    for half in range(halves):
        part = pl.ds(half * width, width)
        sums = pair_sums(count, table, pairs_ref, own_ref.at[:, part], partner_ref.at[:, part])
        if adds:
            rows = pl.ds(half * lots * M, lots * M)
            values, scale = decode(rest[0].at[rows, :], rest[0].at[halves * lots * M :, :], lots, half * lots)
            sums = sums + values * (scale * table[INNER].astype(F32))
        scaled, code = encode(sums)
        coded_ref[half * lots * M : (half + 1) * lots * M, :] = whole(scaled)
        codes += [code[:, lot * LANES : (lot + 1) * LANES] for lot in range(lots)]
    codes += [jnp.zeros((CODE_ROWS - len(codes), LANES), F32)]
    coded_ref[halves * lots * M :, :] = whole(jnp.concatenate(codes, axis=0))


def step(at, swap, layout, scalars, pairs, phases, partner, earlier, after, piece):
    partner, place_in = partner
    local_pairs = phases.shape[0]
    _, blocks, away, _ = layout
    coded_shape = (coded_rows(piece), LANES)
    in_specs = [
        pl.BlockSpec(pairs.shape, lambda i, t, c: (0, 0)),
        pl.BlockSpec((local_pairs, piece), lambda i, t, c: (0, t[blocks + at])),
        pl.BlockSpec((local_pairs, piece), lambda i, t, c: (0, place_in)),
    ]
    operands = [pairs, phases, partner]
    out_shape = [jax.ShapeDtypeStruct(coded_shape, jnp.int16)]
    out_specs = [pl.BlockSpec(coded_shape, lambda i, t, c: (0, 0))]
    if swap is not None:
        first, count = swap
        wide = piece * count
        in_specs.append(pl.BlockSpec((local_pairs, wide), lambda i, t, c: (0, t[away + first] // count)))
        operands.append(phases)
        out_shape.append(jax.ShapeDtypeStruct((local_pairs, wide), phases.dtype))
        out_specs.append(pl.BlockSpec((local_pairs, wide), lambda i, t, c: (0, 0)))
    if earlier is not None:
        in_specs.append(pl.BlockSpec(coded_shape, lambda i, t, c: (0, 0)))
        operands.append(earlier)
    if at in MEETINGS:
        out_shape.append(jax.ShapeDtypeStruct((8, LANES), F32))
        out_specs.append(pl.BlockSpec((8, LANES), lambda i, t, c: (0, 0)))
    in_specs += [pl.BlockSpec(memory_space=pl.ANY)] * len(after)
    results = pl.pallas_call(
        functools.partial(step_kernel, at, layout, earlier is not None, swap is not None, at in MEETINGS, HALVES),
        out_shape=out_shape,
        grid_spec=pltpu.PrefetchScalarGridSpec(
            num_scalar_prefetch=2,
            grid=(1,),
            in_specs=in_specs,
            out_specs=out_specs,
        ),
        compiler_params=pltpu.CompilerParams(vmem_limit_bytes=VMEM_BYTES),
        cost_estimate=STEADY,
        name=f"sum_step_{at:02d}",
    )(*scalars, *operands, *after)
    return results[0], results[1] if swap is not None else None, results[-1] if at in MEETINGS else None


def coded_specs(piece, tiles, index):
    lots = piece // LANES
    return [
        pl.BlockSpec((lots // tiles * M, LANES), lambda *at: (at[index], 0)),
        pl.BlockSpec((CODE_ROWS, LANES), lambda *at: (lots * M // CODE_ROWS, 0)),
    ]


def add_arrived(sums_ref, refs, tiles):
    lots = sums_ref.shape[1] // LANES
    tile = pl.program_id(0)
    for coded_ref, codes_ref in zip(refs[::2], refs[1::2]):
        parts = [decode(coded_ref, codes_ref, lots, at * lots) for at in range(tiles)]
        scale = functools.reduce(lambda chosen, at: jnp.where(tile == at, parts[at][1], chosen), range(1, tiles), parts[0][1])
        sums_ref[...] += parts[0][0] * scale


def finish_kernel(at, layout, tiles, early, table, counts, pairs_ref, own_ref, partner_ref, inverse_ref, *rest):
    out_ref, sums_ref = rest[-2:]
    sums_ref[...] = pair_sums(piece_count(at, layout, table, counts), table, pairs_ref, own_ref, partner_ref)

    @pl.when(table[INNER] == 0)
    def _():
        add_arrived(sums_ref, rest[: 2 * early], tiles)

    @pl.when(table[INNER] == 1)
    def _():
        add_arrived(sums_ref, rest[2 * early : 2 * early + 2 * LATE], tiles)

    out_ref[...] = split_product(inverse_ref[0, :M, :M], sums_ref[...])


def finish(at, part, layout, scalars, pairs, phases, partner, inverse, early, late, series, pixels, piece):
    partner, place_in = partner
    local_pairs = phases.shape[0]
    blocks = layout[1]
    tiles = HALVES
    tile = piece // tiles
    arrived = early + late
    in_specs = [
        pl.BlockSpec(pairs.shape, lambda i, t, c: (0, 0)),
        pl.BlockSpec((local_pairs, tile), lambda i, t, c: (0, t[blocks + at] * tiles + i)),
        pl.BlockSpec((local_pairs, tile), lambda i, t, c: (0, place_in * tiles + i)),
        pl.BlockSpec((1, PAD, PAD), lambda i, t, c: (part // CUTS, 0, 0)),
    ] + coded_specs(piece, tiles, 0) * len(arrived)
    operands = [*scalars, pairs, phases, partner, inverse] + [each for each in arrived for _ in range(2)]
    aliases = {}
    if series is not None:
        in_specs.append(pl.BlockSpec(memory_space=pl.ANY))
        aliases = {len(operands): 0}
        operands.append(series)
    return pl.pallas_call(
        functools.partial(finish_kernel, at, layout, tiles, len(early)),
        out_shape=jax.ShapeDtypeStruct((M, pixels), F32),
        grid_spec=pltpu.PrefetchScalarGridSpec(
            num_scalar_prefetch=2,
            grid=(tiles,),
            in_specs=in_specs,
            out_specs=pl.BlockSpec((M, tile), lambda i, t, c: (0, part * tiles + i)),
            scratch_shapes=[pltpu.VMEM((M, tile), F32)],
        ),
        input_output_aliases=aliases,
        compiler_params=pltpu.CompilerParams(vmem_limit_bytes=VMEM_BYTES),
        cost_estimate=LITTLE,
        name=f"finish_{part}",
    )(*operands)


def line_permutation(links):
    return [(2 * source + side, 2 * target + side) for source, target in links for side in range(2)]


def solve_by_sums(phases, date_pairs, counts_of):
    owner_count = lax.axis_size("ifg")
    line = owner_count // 2
    local_pairs, pixels = phases.shape
    owner_pixels = pixels // owner_count
    runs = counts_of().shape[0]
    parts = runs * CUTS
    piece = owner_pixels // parts
    steps = (line - 1) * parts
    me = lax.axis_index("ifg")

    places = np.repeat(np.array(CHUNK_ORDER), parts, axis=1)
    part_of = np.tile(np.arange(parts), line)
    rows = []
    for device in range(owner_count):
        place, side = device // 2, device % 2
        own = (places[place] * 2 + side) * parts + part_of
        away = (places[place] * 2 + 1 - side) * parts + part_of
        known = [place, line - 1 - place, place ^ 1, line - 1 - (place ^ 1)]
        shift = np.array([known.index(chunk) for chunk in places[place]])
        rows.append(np.concatenate([[device, device ^ 1, int(0 < place < line - 1)], own, away, shift]))
    row = lax.dynamic_index_in_dim(jnp.asarray(np.stack(rows), jnp.int32), me, 0, keepdims=False)
    head, pieces = FIXED, line * parts
    layout = (parts, head, head + pieces, head + 2 * pieces)

    swap = [(i, i ^ 1) for i in range(owner_count)]
    partner_of = {}

    def swapped(away, first, count):
        here = lax.ppermute(away, "ifg", swap)
        partner_of.update({first + place: (here, place) for place in range(count)})

    place, side = me // 2, me % 2
    run_counts = counts_of()
    mirrored = lax.ppermute(run_counts, "ifg", line_permutation([(i, line - 1 - i) for i in range(line)]))
    first, count = FIRST_SWAPS[0]
    chunk, _ = lax.optimization_barrier((jnp.where(place % 2 == 0, line - 1, 0), run_counts))
    away = lax.dynamic_slice(phases, (0, ((chunk * 2 + 1 - side) * parts + first) * piece), (local_pairs, piece * count))
    swapped(away, first, count)
    both = jnp.concatenate([run_counts, mirrored])
    counts = jnp.concatenate([both, lax.ppermute(both, "ifg", line_permutation([(i, i ^ 1) for i in range(line)]))])
    swapped(give_out(FIRST_SWAPS[1], layout, row, phases, mirrored, piece), *FIRST_SWAPS[1])
    pairs = jnp.concatenate([lax.dynamic_slice(date_pairs, (0, row[at] * local_pairs), (2, local_pairs)) for at in (ME, PARTNER)], axis=1)
    scalars = (row, counts)

    received, coded = [], None
    for at in range(steps):
        earlier = received[at - parts][0] if at >= parts else None
        after = [coded] if at else []
        after += received[at - FLIGHT] if at >= FLIGHT else []
        if at - 1 in MEETINGS:
            after.append(met)
        if at in SWAP_WAITS:
            after.append(partner_of[SWAP_WAITS[at]][0])
        if at == INVERSE_STEP:
            inverse = invert_classes(date_pairs, run_counts, [coded])
            after.append(inverse)
        coded, away, told = step(at, SWAPS.get(at), layout, scalars, pairs, phases, partner_of[at], earlier, after, piece)
        received.append([lax.ppermute(coded, "ifg", line_permutation(links)) for links in SENDS[at // parts]])
        if at in SWAPS:
            swapped(away, *SWAPS[at])
        if at in MEETINGS:
            met = lax.ppermute(told, "grp", [(i, i ^ 1) for i in range(lax.axis_size("grp"))])
        if at == 0:
            swapped(give_out(FIRST_SWAPS[2], layout, row, phases, coded, piece), *FIRST_SWAPS[2])

    series = None
    for part in range(parts):
        at = steps + part
        early = [each for place in range(line - 2) for each in received[place * parts + part]]
        late = received[(line - 2) * parts + part]
        series = finish(at, part, layout, scalars, pairs, phases, partner_of[at], inverse, early, late, series, owner_pixels, piece)
    return series


def solve_by_blocks(phases, date_pairs, counts_of):
    owner_count = lax.axis_size("ifg")
    local_pairs, pixels = phases.shape
    owner_pixels = pixels // owner_count
    run_counts = counts_of()
    outgoing = phases.reshape(local_pairs, owner_count, owner_pixels).transpose(1, 0, 2)
    received = lax.all_to_all(outgoing, "ifg", split_axis=0, concat_axis=0, tiled=True)
    inverse = invert_classes(date_pairs, run_counts, [])
    return sum_solve(run_counts, date_pairs, received.reshape(-1, owner_pixels), inverse)


def local(phases, date_pairs, pair_counts, group_ids):
    local_pairs, _, pixels = phases.shape

    def counts_of():
        strip_groups = lax.dynamic_index_in_dim(group_ids, lax.axis_index("grp"), 0, keepdims=False)[::RUN]
        chosen = strip_groups[:, None] == jnp.arange(pair_counts.shape[0], dtype=jnp.int32)
        return jnp.sum(jnp.where(chosen, pair_counts, 0), axis=1)

    line = lax.axis_size("ifg") == 2 * len(CHUNK_ORDER) and group_ids.shape[1] == 2 * RUN
    by_sums = line and 2 * local_pairs > M and local_pairs % LANES == 0 and lax.axis_size("grp") % 2 == 0
    solve = solve_by_sums if by_sums else solve_by_blocks
    return solve(phases.reshape(local_pairs, pixels), date_pairs, counts_of)[None, :, :]


def solution(mesh):
    in_specs = (P("ifg", "grp", None), P(), P(), P(None, "ifg"))
    out_specs = P("grp", None, "ifg")
    return jax.shard_map(local, mesh=mesh, in_specs=in_specs, out_specs=out_specs, check_vma=False)
```

profile of v0, /device:TPU:0, one launch (start us, length us, event | category | flops | bytes accessed | tf_op | source)
XLA Modules:
  0.0 146.6 jit_solution(11420093165276470950)
XLA Ops:
  0.8 0.8 fusion.counts_ref
  1.6 5.1 %collective-permute-start = (s32[2]{0:T(128)S(1)}, s32[2]{0:T(128)S(1)}, u32[]{:S(2)}, u32[]{:S(2)}) collective-permute-start(s32[2]{0:T(128)S(1)} %fusion.counts_ref), channel_id=1, source_target_pairs={{0,24},{4,28},{8,16},{12,20},{16,8},{20,12},{24,0},{28,4},{1,25},{... | collective-permute-start | bytes 32 | tf_op jit(solution)/shard_map/ppermute | solution.py:393
  6.7 1.0 dynamic-slice_bitcast_fusion
  7.7 1.6 %collective-permute-start.2 = (bf16[128,1024]{1,0:T(8,128)(2,1)S(1)}, bf16[128,1024]{1,0:T(8,128)(2,1)S(1)}, u32[]{:S(2)}, u32[]{:S(2)}) collective-permute-start(bf16[128,1024]{1,0:T(8,128)(2,1)S(1)} %dynamic-slice_bitcast_fusion), channel_id=1, source_target_pairs={{0,4},{4,0},{8,12},{12,8},{16,20},{20,16},{24,28},{28,24},{1,5},{5... | collective-permute-start | bytes 786440 | tf_op jit(solution)/shard_map/ppermute | solution.py:388
  9.3 0.7 constant_dynamic-slice_fusion.3
  11.8 0.7 constant_dynamic-slice_fusion.1
  12.6 1.5 %give_out.3 = bf16[128,1024]{1,0:T(8,128)(2,1)S(1)} custom-call(s32[51]{0:T(128)S(1)} %get-tuple-element.48.table, bf16[128,32768]{1,0:T(8,128)(2,1)} %bitcast.10, s32[2]{0:T(128)S(1)} %collective-permute-done._), custom_call_target="tpu_custom_call" | custom-call | flops 1024 | bytes 1024 | tf_op jit(solution)/shard_map/give_out/pallas_call | solution.py:199
  14.7 1.4 collective-permute-done.1
  16.2 2.0 %sum_step_00.1._.rest_0_ = s16[1616,128]{1,0:T(8,128)(2,1)S(1)} custom-call(s32[51]{0:T(128)S(1)} %get-tuple-element.48.table, s32[8]{0:T(128)S(1)} %pad_add_fusion.2.counts, s32[2,256]{1,0:T(2,128)S(1)} %pad_add_fusion.pairs_ref, bf16[128,32768]{1,0:T(8,128)(2,1)} %bitcast.11, bf16[128,1024]{1,0:T(8,128)(2,1)S(1)} %collective-permute-done.2.partner_ref), custom_call_target="tpu_custom_call" | custom-call | flops 10000000000 | bytes 30000000 | tf_op jit(solution)/shard_map/sum_step_00/pallas_call | solution.py:271
  18.8 1.6 %give_out.2 = bf16[128,2048]{1,0:T(8,128)(2,1)S(1)} custom-call(s32[51]{0:T(128)S(1)} %get-tuple-element.48.table, bf16[128,32768]{1,0:T(8,128)(2,1)} %bitcast.12, s16[1616,128]{1,0:T(8,128)(2,1)S(1)} %sum_step_00.1._.rest_0_), custom_call_target="tpu_custom_call" | custom-call | flops 1024 | bytes 1024 | tf_op jit(solution)/shard_map/give_out/pallas_call | solution.py:199
  20.5 1.6 %collective-permute-start.3 = (bf16[128,2048]{1,0:T(8,128)(2,1)S(1)}, bf16[128,2048]{1,0:T(8,128)(2,1)S(1)}, u32[]{:S(2)}, u32[]{:S(2)}) collective-permute-start(bf16[128,2048]{1,0:T(8,128)(2,1)S(1)} %give_out.2), channel_id=1, source_target_pairs={{0,4},{4,0},{8,12},{12,8},{16,20},{20,16},{24,28},{28,24},{1,5},{5... | collective-permute-start | bytes 1572872 | tf_op jit(solution)/shard_map/ppermute | solution.py:388
  22.0 2.0 %sum_step_01.1 = (s16[1616,128]{1,0:T(8,128)(2,1)S(1)}, f32[8,128]{1,0:T(8,128)S(1)}) custom-call(s32[51]{0:T(128)S(1)} %get-tuple-element.48.table, s32[8]{0:T(128)S(1)} %pad_add_fusion.2.counts, s32[2,256]{1,0:T(2,128)S(1)} %pad_add_fusion.pairs_ref, bf16[128,32768]{1,0:T(8,128)(2,1)} %bitcast.13, ...), custom_call_target="tpu_custom_call" | custom-call | flops 10000000000 | bytes 30000000 | tf_op jit(solution)/shard_map/sum_step_01/pallas_call | solution.py:271
  24.1 2.0 %collective-permute-start.7 = (s16[1616,128]{1,0:T(8,128)(2,1)S(1)}, s16[1616,128]{1,0:T(8,128)(2,1)S(1)}, u32[]{:S(2)}, u32[]{:S(2)}) collective-permute-start(s16[1616,128]{1,0:T(8,128)(2,1)S(1)} %get-tuple-element.26.rest_0_.rest_1_), channel_id=1, source_target_pairs={{0,8},{4,12},{8,0},{12,4},{16,24},{20,28},{24,16},{28,20},{1,9},{5... | collective-permute-start | bytes 1241096 | tf_op jit(solution)/shard_map/ppermute | solution.py:417
  26.1 6.8 %invert_classes_0.1.rest_4_.inverse_ref = f32[2,256,256]{2,1,0:T(8,128)S(1)} custom-call(s32[2]{0:T(128)S(1)} %fusion.counts_ref, s32[2,1024]{1,0:T(2,128)S(1)} %copy-done.1, s16[1616,128]{1,0:T(8,128)(2,1)S(1)} %get-tuple-element.26.rest_0_.rest_1_), custom_call_target="tpu_custom_call" | custom-call | flops 1024 | bytes 1024 | tf_op jit(solution)/shard_map/invert_classes_0/pallas_call | solution.py:103
  32.9 2.2 %sum_step_02.1 = (s16[1616,128]{1,0:T(8,128)(2,1)S(1)}, bf16[128,2048]{1,0:T(8,128)(2,1)S(1)}) custom-call(s32[51]{0:T(128)S(1)} %get-tuple-element.48.table, s32[8]{0:T(128)S(1)} %pad_add_fusion.2.counts, s32[2,256]{1,0:T(2,128)S(1)} %pad_add_fusion.pairs_ref, bf16[128,32768]{1,0:T(8,128)(2,1)} %bitcast.14, ...), custom_call_target="tpu_custom_call" | custom-call | flops 10000000000 | bytes 30000000 | tf_op jit(solution)/shard_map/sum_step_02/pallas_call | solution.py:271
  35.1 1.7 %collective-permute-start.10 = (s16[1616,128]{1,0:T(8,128)(2,1)S(1)}, s16[1616,128]{1,0:T(8,128)(2,1)S(1)}, u32[]{:S(2)}, u32[]{:S(2)}) collective-permute-start(s16[1616,128]{1,0:T(8,128)(2,1)S(1)} %get-tuple-element.28.rest_1_), channel_id=1, source_target_pairs={{0,8},{4,12},{8,0},{12,4},{16,24},{20,28},{24,16},{28,20},{1,9},{5... | collective-permute-start | bytes 1241096 | tf_op jit(solution)/shard_map/ppermute | solution.py:417
  37.4 2.2 %sum_step_03.1 = (s16[1616,128]{1,0:T(8,128)(2,1)S(1)}, bf16[128,2048]{1,0:T(8,128)(2,1)S(1)}, f32[8,128]{1,0:T(8,128)S(1)}) custom-call(s32[51]{0:T(128)S(1)} %get-tuple-element.48.table, s32[8]{0:T(128)S(1)} %pad_add_fusion.2.counts, s32[2,256]{1,0:T(2,128)S(1)} %pad_add_fusion.pairs_ref, bf16[128,32768]{1,0:T(8,128)(2,1)} %bitcast.16, ...), custom_call_target="tpu_custom_call" | custom-call | flops 10000000000 | bytes 30000000 | tf_op jit(solution)/shard_map/sum_step_03/pallas_call | solution.py:271
  39.6 1.2 collective-permute-start.9
  40.9 1.1 collective-permute-start.8
  41.9 5.7 %collective-permute-done.10.rest_2_.rest_1_.rest_0_ = s16[1616,128]{1,0:T(8,128)(2,1)S(1)} collective-permute-done((s16[1616,128]{1,0:T(8,128)(2,1)S(1)}, s16[1616,128]{1,0:T(8,128)(2,1)S(1)}, u32[]{:S(2)}, u32[]{:S(2)}) %collective-permute-start.10) | collective-permute-done | bytes 413728 | tf_op jit(solution)/shard_map/ppermute | solution.py:417
  47.6 4.1 %collective-permute-done.11.partner_ref = bf16[128,2048]{1,0:T(8,128)(2,1)S(1)} collective-permute-done((bf16[128,2048]{1,0:T(8,128)(2,1)S(1)}, bf16[128,2048]{1,0:T(8,128)(2,1)S(1)}, u32[]{:S(2)}, u32[]{:S(2)}) %collective-permute-start.11) | collective-permute-done | bytes 524320 | tf_op jit(solution)/shard_map/ppermute | solution.py:388
  51.7 2.0 %sum_step_04.1.rest_2_ = s16[1616,128]{1,0:T(8,128)(2,1)S(1)} custom-call(s32[51]{0:T(128)S(1)} %get-tuple-element.48.table, s32[8]{0:T(128)S(1)} %pad_add_fusion.2.counts, s32[2,256]{1,0:T(2,128)S(1)} %pad_add_fusion.pairs_ref, bf16[128,32768]{1,0:T(8,128)(2,1)} %bitcast.18, bf16[128,2048]{1,0:T(8,128)(2,1)S(1)} %collective-permute-done.11.partner_ref, ...), custom_call_target="tpu_custom_call" | custom-call | flops 10000000000 | bytes 30000000 | tf_op jit(solution)/shard_map/sum_step_04/pallas_call | solution.py:271
  54.1 11.3 %collective-permute-done.9.rest_3_.rest_1_.rest_0_ = s16[1616,128]{1,0:T(8,128)(2,1)S(1)} collective-permute-done((s16[1616,128]{1,0:T(8,128)(2,1)S(1)}, s16[1616,128]{1,0:T(8,128)(2,1)S(1)}, u32[]{:S(2)}, u32[]{:S(2)}) %collective-permute-start.9) | collective-permute-done | bytes 413728 | tf_op jit(solution)/shard_map/ppermute | solution.py:417
  65.3 2.2 %sum_step_05.1 = (s16[1616,128]{1,0:T(8,128)(2,1)S(1)}, bf16[128,2048]{1,0:T(8,128)(2,1)S(1)}, f32[8,128]{1,0:T(8,128)S(1)}) custom-call(s32[51]{0:T(128)S(1)} %get-tuple-element.48.table, s32[8]{0:T(128)S(1)} %pad_add_fusion.2.counts, s32[2,256]{1,0:T(2,128)S(1)} %pad_add_fusion.pairs_ref, bf16[128,32768]{1,0:T(8,128)(2,1)} %bitcast.20, ...), custom_call_target="tpu_custom_call" | custom-call | flops 10000000000 | bytes 30000000 | tf_op jit(solution)/shard_map/sum_step_05/pallas_call | solution.py:271
  67.8 1.0 collective-permute-done.14.rest_4_
  68.8 2.2 %sum_step_06.1 = (s16[1616,128]{1,0:T(8,128)(2,1)S(1)}, bf16[128,2048]{1,0:T(8,128)(2,1)S(1)}) custom-call(s32[51]{0:T(128)S(1)} %get-tuple-element.48.table, s32[8]{0:T(128)S(1)} %pad_add_fusion.2.counts, s32[2,256]{1,0:T(2,128)S(1)} %pad_add_fusion.pairs_ref, bf16[128,32768]{1,0:T(8,128)(2,1)} %bitcast.21, ...), custom_call_target="tpu_custom_call" | custom-call | flops 10000000000 | bytes 30000000 | tf_op jit(solution)/shard_map/sum_step_06/pallas_call | solution.py:271
  71.1 1.1 collective-permute-start.19
  72.1 8.8 %collective-permute-done.15.rest_3_.rest_0_.rest_2_ = s16[1616,128]{1,0:T(8,128)(2,1)S(1)} collective-permute-done((s16[1616,128]{1,0:T(8,128)(2,1)S(1)}, s16[1616,128]{1,0:T(8,128)(2,1)S(1)}, u32[]{:S(2)}, u32[]{:S(2)}) %collective-permute-start.15) | collective-permute-done | bytes 413728 | tf_op jit(solution)/shard_map/ppermute | solution.py:417
  81.0 1.5 %collective-permute-done.16.rest_4_.partner_ref = bf16[128,2048]{1,0:T(8,128)(2,1)S(1)} collective-permute-done((bf16[128,2048]{1,0:T(8,128)(2,1)S(1)}, bf16[128,2048]{1,0:T(8,128)(2,1)S(1)}, u32[]{:S(2)}, u32[]{:S(2)}) %collective-permute-start.16) | collective-permute-done | bytes 524320 | tf_op jit(solution)/shard_map/ppermute | solution.py:388
  82.5 2.4 %sum_step_07.1 = (s16[1616,128]{1,0:T(8,128)(2,1)S(1)}, bf16[128,4096]{1,0:T(8,128)(2,1)S(1)}, f32[8,128]{1,0:T(8,128)S(1)}) custom-call(s32[51]{0:T(128)S(1)} %get-tuple-element.48.table, s32[8]{0:T(128)S(1)} %pad_add_fusion.2.counts, s32[2,256]{1,0:T(2,128)S(1)} %pad_add_fusion.pairs_ref, bf16[128,32768]{1,0:T(8,128)(2,1)} %bitcast.23, ...), custom_call_target="tpu_custom_call" | custom-call | flops 10000000000 | bytes 30000000 | tf_op jit(solution)/shard_map/sum_step_07/pallas_call | solution.py:271
  85.2 0.9 collective-permute-done.21.rest_3_
  86.2 3.2 %collective-permute-done.20.rest_2_.rest_0_.rest_3_ = s16[1616,128]{1,0:T(8,128)(2,1)S(1)} collective-permute-done((s16[1616,128]{1,0:T(8,128)(2,1)S(1)}, s16[1616,128]{1,0:T(8,128)(2,1)S(1)}, u32[]{:S(2)}, u32[]{:S(2)}) %collective-permute-start.20) | collective-permute-done | bytes 413728 | tf_op jit(solution)/shard_map/ppermute | solution.py:417
  89.4 4.4 %collective-permute-done.19.rest_4_.partner_ref = bf16[128,2048]{1,0:T(8,128)(2,1)S(1)} collective-permute-done((bf16[128,2048]{1,0:T(8,128)(2,1)S(1)}, bf16[128,2048]{1,0:T(8,128)(2,1)S(1)}, u32[]{:S(2)}, u32[]{:S(2)}) %collective-permute-start.19) | collective-permute-done | bytes 524320 | tf_op jit(solution)/shard_map/ppermute | solution.py:388
  93.7 2.0 %sum_step_08.1 = (s16[1616,128]{1,0:T(8,128)(2,1)S(1)}, f32[8,128]{1,0:T(8,128)S(1)}) custom-call(s32[51]{0:T(128)S(1)} %get-tuple-element.48.table, s32[8]{0:T(128)S(1)} %pad_add_fusion.2.counts, s32[2,256]{1,0:T(2,128)S(1)} %pad_add_fusion.pairs_ref, bf16[128,32768]{1,0:T(8,128)(2,1)} %bitcast.25, ...), custom_call_target="tpu_custom_call" | custom-call | flops 10000000000 | bytes 30000000 | tf_op jit(solution)/shard_map/sum_step_08/pallas_call | solution.py:271
  96.5 6.6 %collective-permute-start.23 = (s16[1616,128]{1,0:T(8,128)(2,1)S(1)}, s16[1616,128]{1,0:T(8,128)(2,1)S(1)}, u32[]{:S(2)}, u32[]{:S(2)}) collective-permute-start(s16[1616,128]{1,0:T(8,128)(2,1)S(1)} %get-tuple-element.41.rest_1_), channel_id=1, source_target_pairs={{0,8},{4,12},{24,16},{28,20},{1,9},{5,13},{25,17},{29,21},{2,10},{... | collective-permute-start | bytes 1241096 | tf_op jit(solution)/shard_map/ppermute | solution.py:417
  103.2 2.0 %sum_step_09.1.rest_1_ = s16[1616,128]{1,0:T(8,128)(2,1)S(1)} custom-call(s32[51]{0:T(128)S(1)} %get-tuple-element.48.table, s32[8]{0:T(128)S(1)} %pad_add_fusion.2.counts, s32[2,256]{1,0:T(2,128)S(1)} %pad_add_fusion.pairs_ref, bf16[128,32768]{1,0:T(8,128)(2,1)} %bitcast.26, bf16[128,2048]{1,0:T(8,128)(2,1)S(1)} %collective-permute-done.16.rest_4_.partner_ref, ...), custom_call_target="tpu_custom_call" | custom-call | flops 10000000000 | bytes 30000000 | tf_op jit(solution)/shard_map/sum_step_09/pallas_call | solution.py:271
  105.9 2.5 %collective-permute-start.25 = (s16[1616,128]{1,0:T(8,128)(2,1)S(1)}, s16[1616,128]{1,0:T(8,128)(2,1)S(1)}, u32[]{:S(2)}, u32[]{:S(2)}) collective-permute-start(s16[1616,128]{1,0:T(8,128)(2,1)S(1)} %sum_step_09.1.rest_1_), channel_id=1, source_target_pairs={{0,8},{4,12},{24,16},{28,20},{1,9},{5,13},{25,17},{29,21},{2,10},{... | collective-permute-start | bytes 1241096 | tf_op jit(solution)/shard_map/ppermute | solution.py:417
  108.4 4.6 %collective-permute-done.23.rest_2_.rest_4_.rest_5_ = s16[1616,128]{1,0:T(8,128)(2,1)S(1)} collective-permute-done((s16[1616,128]{1,0:T(8,128)(2,1)S(1)}, s16[1616,128]{1,0:T(8,128)(2,1)S(1)}, u32[]{:S(2)}, u32[]{:S(2)}) %collective-permute-start.23) | collective-permute-done | bytes 413728 | tf_op jit(solution)/shard_map/ppermute | solution.py:417
  113.0 2.6 %collective-permute-done.17.rest_4_.partner_ref = bf16[128,4096]{1,0:T(8,128)(2,1)S(1)} collective-permute-done((bf16[128,4096]{1,0:T(8,128)(2,1)S(1)}, bf16[128,4096]{1,0:T(8,128)(2,1)S(1)}, u32[]{:S(2)}, u32[]{:S(2)}) %collective-permute-start.17) | collective-permute-done | bytes 1048608 | tf_op jit(solution)/shard_map/ppermute | solution.py:388
  115.7 2.0 %sum_step_10.1 = (s16[1616,128]{1,0:T(8,128)(2,1)S(1)}, f32[8,128]{1,0:T(8,128)S(1)}) custom-call(s32[51]{0:T(128)S(1)} %get-tuple-element.48.table, s32[8]{0:T(128)S(1)} %pad_add_fusion.2.counts, s32[2,256]{1,0:T(2,128)S(1)} %pad_add_fusion.pairs_ref, bf16[128,32768]{1,0:T(8,128)(2,1)} %bitcast.27, ...), custom_call_target="tpu_custom_call" | custom-call | flops 10000000000 | bytes 30000000 | tf_op jit(solution)/shard_map/sum_step_10/pallas_call | solution.py:271
  118.4 6.4 %collective-permute-start.30 = (s16[1616,128]{1,0:T(8,128)(2,1)S(1)}, s16[1616,128]{1,0:T(8,128)(2,1)S(1)}, u32[]{:S(2)}, u32[]{:S(2)}) collective-permute-start(s16[1616,128]{1,0:T(8,128)(2,1)S(1)} %get-tuple-element.43.rest_1_), channel_id=1, source_target_pairs={{0,8},{4,12},{24,16},{28,20},{1,9},{5,13},{25,17},{29,21},{2,10},{... | collective-permute-start | bytes 1241096 | tf_op jit(solution)/shard_map/ppermute | solution.py:417
  124.9 2.0 %sum_step_11.1 = s16[1616,128]{1,0:T(8,128)(2,1)S(1)} custom-call(s32[51]{0:T(128)S(1)} %get-tuple-element.48.table, s32[8]{0:T(128)S(1)} %pad_add_fusion.2.counts, s32[2,256]{1,0:T(2,128)S(1)} %pad_add_fusion.pairs_ref, bf16[128,32768]{1,0:T(8,128)(2,1)} %bitcast.28, bf16[128,2048]{1,0:T(8,128)(2,1)S(1)} %collective-permute-done.19.rest_4_.partner_ref, ...), custom_call_target="tpu_custom_call" | custom-call | flops 10000000000 | bytes 30000000 | tf_op jit(solution)/shard_map/sum_step_11/pallas_call | solution.py:271
  127.6 2.7 %collective-permute-start.28 = (s16[1616,128]{1,0:T(8,128)(2,1)S(1)}, s16[1616,128]{1,0:T(8,128)(2,1)S(1)}, u32[]{:S(2)}, u32[]{:S(2)}) collective-permute-start(s16[1616,128]{1,0:T(8,128)(2,1)S(1)} %sum_step_11.1), channel_id=1, source_target_pairs={{0,8},{4,12},{24,16},{28,20},{1,9},{5,13},{25,17},{29,21},{2,10},{... | collective-permute-start | bytes 1241096 | tf_op jit(solution)/shard_map/ppermute | solution.py:417
  130.3 3.7 %finish_0.1.rest_8_ = f32[200,4096]{1,0:T(8,128)} custom-call(s32[51]{0:T(128)S(1)} %get-tuple-element.48.table, s32[8]{0:T(128)S(1)} %pad_add_fusion.2.counts, s32[2,256]{1,0:T(2,128)S(1)} %pad_add_fusion.pairs_ref, bf16[128,32768]{1,0:T(8,128)(2,1)} %bitcast.29, bf16[128,4096]{1,0:T(8,128)(2,1)S(1)} %collective-permute-done.17.rest_4_.partner_ref, ...), custom_call_target="tpu_custom_call" | custom-call | flops 1024 | bytes 1024 | tf_op jit(solution)/shard_map/finish_0/pallas_call | solution.py:338
  134.0 3.7 %finish_1.1.rest_8_ = f32[200,4096]{1,0:T(8,128)} custom-call(s32[51]{0:T(128)S(1)} %get-tuple-element.48.table, s32[8]{0:T(128)S(1)} %pad_add_fusion.2.counts, s32[2,256]{1,0:T(2,128)S(1)} %pad_add_fusion.pairs_ref, bf16[128,32768]{1,0:T(8,128)(2,1)} %bitcast.30, ...), custom_call_target="tpu_custom_call", output_to_operand_aliasing={{}: (14, {})} | custom-call | flops 1024 | bytes 1024 | tf_op jit(solution)/shard_map/finish_1/pallas_call | solution.py:338
  137.8 3.7 %finish_2.1.rest_8_ = f32[200,4096]{1,0:T(8,128)} custom-call(s32[51]{0:T(128)S(1)} %get-tuple-element.48.table, s32[8]{0:T(128)S(1)} %pad_add_fusion.2.counts, s32[2,256]{1,0:T(2,128)S(1)} %pad_add_fusion.pairs_ref, bf16[128,32768]{1,0:T(8,128)(2,1)} %bitcast.31, ...), custom_call_target="tpu_custom_call", output_to_operand_aliasing={{}: (14, {})} | custom-call | flops 1024 | bytes 1024 | tf_op jit(solution)/shard_map/finish_2/pallas_call | solution.py:338
  141.5 1.3 collective-permute-done.28.rest_4_.rest_5_
  142.8 3.7 %finish_3.1 = f32[200,4096]{1,0:T(8,128)} custom-call(s32[51]{0:T(128)S(1)} %get-tuple-element.48.table, s32[8]{0:T(128)S(1)} %pad_add_fusion.2.counts, s32[2,256]{1,0:T(2,128)S(1)} %pad_add_fusion.pairs_ref, bf16[128,32768]{1,0:T(8,128)(2,1)} %bitcast.32, ...), custom_call_target="tpu_custom_call", output_to_operand_aliasing={{}: (14, {})} | custom-call | flops 1024 | bytes 1024 | tf_op jit(solution)/shard_map/finish_3/pallas_call | solution.py:338
  (49 shorter events, 7.3 us)
Async XLA Ops:
  0.0 0.7 copy-start
  1.6 10.9 %collective-permute-start = (s32[2]{0:T(128)S(1)}, s32[2]{0:T(128)S(1)}, u32[]{:S(2)}, u32[]{:S(2)}) collective-permute-start(s32[2]{0:T(128)S(1)} %fusion.counts_ref), channel_id=1, source_target_pairs={{0,24},{4,28},{8,16},{12,20},{16,8},{20,12},{24,0},{28,4},{1,25},{... | collective-permute-start | bytes 32 | tf_op jit(solution)/shard_map/ppermute | solution.py:393
  7.7 8.5 %collective-permute-start.2 = (bf16[128,1024]{1,0:T(8,128)(2,1)S(1)}, bf16[128,1024]{1,0:T(8,128)(2,1)S(1)}, u32[]{:S(2)}, u32[]{:S(2)}) collective-permute-start(bf16[128,1024]{1,0:T(8,128)(2,1)S(1)} %dynamic-slice_bitcast_fusion), channel_id=1, source_target_pairs={{0,4},{4,0},{8,12},{12,8},{16,20},{20,16},{24,28},{28,24},{1,5},{5... | collective-permute-start | bytes 786440 | tf_op jit(solution)/shard_map/ppermute | solution.py:388
  12.6 3.5 %collective-permute-start.1 = (s32[4]{0:T(128)S(1)}, s32[4]{0:T(128)S(1)}, u32[]{:S(2)}, u32[]{:S(2)}) collective-permute-start(s32[4]{0:T(128)S(1)} %pad_add_fusion.1), channel_id=1, source_target_pairs={{0,8},{4,12},{8,0},{12,4},{16,24},{20,28},{24,16},{28,20},{1,9},{5... | collective-permute-start | bytes 56 | tf_op jit(solution)/shard_map/ppermute | solution.py:399
  14.1 7.9 %collective-permute-start.4 = (bf16[128,1024]{1,0:T(8,128)(2,1)S(1)}, bf16[128,1024]{1,0:T(8,128)(2,1)S(1)}, u32[]{:S(2)}, u32[]{:S(2)}) collective-permute-start(bf16[128,1024]{1,0:T(8,128)(2,1)S(1)} %give_out.3), channel_id=1, source_target_pairs={{0,4},{4,0},{8,12},{12,8},{16,20},{20,16},{24,28},{28,24},{1,5},{5... | collective-permute-start | bytes 786440 | tf_op jit(solution)/shard_map/ppermute | solution.py:388
  18.2 14.8 %collective-permute-start.5 = (s16[1616,128]{1,0:T(8,128)(2,1)S(1)}, s16[1616,128]{1,0:T(8,128)(2,1)S(1)}, u32[]{:S(2)}, u32[]{:S(2)}) collective-permute-start(s16[1616,128]{1,0:T(8,128)(2,1)S(1)} %sum_step_00.1._.rest_0_), channel_id=1, source_target_pairs={{0,8},{4,12},{8,0},{12,4},{16,24},{20,28},{24,16},{28,20},{1,9},{5... | collective-permute-start | bytes 1241096 | tf_op jit(solution)/shard_map/ppermute | solution.py:417
  20.4 5.7 %copy-start.1 = (s32[2,1024]{1,0:T(2,128)S(1)}, s32[2,1024]{1,0:T(2,128)}, u32[]{:S(2)}) copy-start(s32[2,1024]{1,0:T(2,128)} %pairs_ref.1) | copy-start | bytes 24580
  20.5 12.5 %collective-permute-start.3 = (bf16[128,2048]{1,0:T(8,128)(2,1)S(1)}, bf16[128,2048]{1,0:T(8,128)(2,1)S(1)}, u32[]{:S(2)}, u32[]{:S(2)}) collective-permute-start(bf16[128,2048]{1,0:T(8,128)(2,1)S(1)} %give_out.2), channel_id=1, source_target_pairs={{0,4},{4,0},{8,12},{12,8},{16,20},{20,16},{24,28},{28,24},{1,5},{5... | collective-permute-start | bytes 1572872 | tf_op jit(solution)/shard_map/ppermute | solution.py:388
  24.0 8.9 %collective-permute-start.6 = (f32[8,128]{1,0:T(8,128)S(1)}, f32[8,128]{1,0:T(8,128)S(1)}, u32[]{:S(2)}, u32[]{:S(2)}) collective-permute-start(f32[8,128]{1,0:T(8,128)S(1)} %get-tuple-element.27), channel_id=1, source_target_pairs={{0,1},{1,0},{2,3},{3,2},{4,5},{5,4},{6,7},{7,6},{8,9},{9,8},{10,11... | collective-permute-start | bytes 12296 | tf_op jit(solution)/shard_map/ppermute | solution.py:421
  24.1 13.3 %collective-permute-start.7 = (s16[1616,128]{1,0:T(8,128)(2,1)S(1)}, s16[1616,128]{1,0:T(8,128)(2,1)S(1)}, u32[]{:S(2)}, u32[]{:S(2)}) collective-permute-start(s16[1616,128]{1,0:T(8,128)(2,1)S(1)} %get-tuple-element.26.rest_0_.rest_1_), channel_id=1, source_target_pairs={{0,8},{4,12},{8,0},{12,4},{16,24},{20,28},{24,16},{28,20},{1,9},{5... | collective-permute-start | bytes 1241096 | tf_op jit(solution)/shard_map/ppermute | solution.py:417
  35.1 12.5 %collective-permute-start.10 = (s16[1616,128]{1,0:T(8,128)(2,1)S(1)}, s16[1616,128]{1,0:T(8,128)(2,1)S(1)}, u32[]{:S(2)}, u32[]{:S(2)}) collective-permute-start(s16[1616,128]{1,0:T(8,128)(2,1)S(1)} %get-tuple-element.28.rest_1_), channel_id=1, source_target_pairs={{0,8},{4,12},{8,0},{12,4},{16,24},{20,28},{24,16},{28,20},{1,9},{5... | collective-permute-start | bytes 1241096 | tf_op jit(solution)/shard_map/ppermute | solution.py:417
  36.9 14.9 %collective-permute-start.11 = (bf16[128,2048]{1,0:T(8,128)(2,1)S(1)}, bf16[128,2048]{1,0:T(8,128)(2,1)S(1)}, u32[]{:S(2)}, u32[]{:S(2)}) collective-permute-start(bf16[128,2048]{1,0:T(8,128)(2,1)S(1)} %get-tuple-element.31), channel_id=1, source_target_pairs={{0,4},{4,0},{8,12},{12,8},{16,20},{20,16},{24,28},{28,24},{1,5},{5... | collective-permute-start | bytes 1572872 | tf_op jit(solution)/shard_map/ppermute | solution.py:388
  39.6 2.4 %collective-permute-start.12 = (f32[8,128]{1,0:T(8,128)S(1)}, f32[8,128]{1,0:T(8,128)S(1)}, u32[]{:S(2)}, u32[]{:S(2)}) collective-permute-start(f32[8,128]{1,0:T(8,128)S(1)} %get-tuple-element.32), channel_id=1, source_target_pairs={{0,1},{1,0},{2,3},{3,2},{4,5},{5,4},{6,7},{7,6},{8,9},{9,8},{10,11... | collective-permute-start | bytes 12296 | tf_op jit(solution)/shard_map/ppermute | solution.py:421
  39.6 25.7 %collective-permute-start.9 = (s16[1616,128]{1,0:T(8,128)(2,1)S(1)}, s16[1616,128]{1,0:T(8,128)(2,1)S(1)}, u32[]{:S(2)}, u32[]{:S(2)}) collective-permute-start(s16[1616,128]{1,0:T(8,128)(2,1)S(1)} %get-tuple-element.30.rest_1_), channel_id=1, source_target_pairs={{0,8},{4,12},{8,0},{12,4},{16,24},{20,28},{24,16},{28,20},{1,9},{5... | collective-permute-start | bytes 1241096 | tf_op jit(solution)/shard_map/ppermute | solution.py:417
  40.9 24.5 %collective-permute-start.8 = (bf16[128,2048]{1,0:T(8,128)(2,1)S(1)}, bf16[128,2048]{1,0:T(8,128)(2,1)S(1)}, u32[]{:S(2)}, u32[]{:S(2)}) collective-permute-start(bf16[128,2048]{1,0:T(8,128)(2,1)S(1)} %get-tuple-element.29), channel_id=1, source_target_pairs={{0,4},{4,0},{8,12},{12,8},{16,20},{20,16},{24,28},{28,24},{1,5},{5... | collective-permute-start | bytes 1572872 | tf_op jit(solution)/shard_map/ppermute | solution.py:388
  53.7 15.1 %collective-permute-start.13 = (s16[1616,128]{1,0:T(8,128)(2,1)S(1)}, s16[1616,128]{1,0:T(8,128)(2,1)S(1)}, u32[]{:S(2)}, u32[]{:S(2)}) collective-permute-start(s16[1616,128]{1,0:T(8,128)(2,1)S(1)} %sum_step_04.1.rest_2_), channel_id=1, source_target_pairs={{0,8},{4,12},{8,24},{12,28},{16,0},{20,4},{24,16},{28,20},{1,9},{5... | collective-permute-start | bytes 1241096 | tf_op jit(solution)/shard_map/ppermute | solution.py:417
  67.5 1.2 collective-permute-start.14
  67.7 13.3 %collective-permute-start.15 = (s16[1616,128]{1,0:T(8,128)(2,1)S(1)}, s16[1616,128]{1,0:T(8,128)(2,1)S(1)}, u32[]{:S(2)}, u32[]{:S(2)}) collective-permute-start(s16[1616,128]{1,0:T(8,128)(2,1)S(1)} %get-tuple-element.33.rest_2_), channel_id=1, source_target_pairs={{0,8},{4,12},{8,24},{12,28},{16,0},{20,4},{24,16},{28,20},{1,9},{5... | collective-permute-start | bytes 1241096 | tf_op jit(solution)/shard_map/ppermute | solution.py:417
  67.7 14.8 %collective-permute-start.16 = (bf16[128,2048]{1,0:T(8,128)(2,1)S(1)}, bf16[128,2048]{1,0:T(8,128)(2,1)S(1)}, u32[]{:S(2)}, u32[]{:S(2)}) collective-permute-start(bf16[128,2048]{1,0:T(8,128)(2,1)S(1)} %get-tuple-element.36), channel_id=1, source_target_pairs={{0,4},{4,0},{8,12},{12,8},{16,20},{20,16},{24,28},{28,24},{1,5},{5... | collective-permute-start | bytes 1572872 | tf_op jit(solution)/shard_map/ppermute | solution.py:388
  71.0 18.4 %collective-permute-start.20 = (s16[1616,128]{1,0:T(8,128)(2,1)S(1)}, s16[1616,128]{1,0:T(8,128)(2,1)S(1)}, u32[]{:S(2)}, u32[]{:S(2)}) collective-permute-start(s16[1616,128]{1,0:T(8,128)(2,1)S(1)} %get-tuple-element.35.rest_2_), channel_id=1, source_target_pairs={{0,8},{4,12},{8,24},{12,28},{16,0},{20,4},{24,16},{28,20},{1,9},{5... | collective-permute-start | bytes 1241096 | tf_op jit(solution)/shard_map/ppermute | solution.py:417
  71.1 22.7 %collective-permute-start.19 = (bf16[128,2048]{1,0:T(8,128)(2,1)S(1)}, bf16[128,2048]{1,0:T(8,128)(2,1)S(1)}, u32[]{:S(2)}, u32[]{:S(2)}) collective-permute-start(bf16[128,2048]{1,0:T(8,128)(2,1)S(1)} %get-tuple-element.39), channel_id=1, source_target_pairs={{0,4},{4,0},{8,12},{12,8},{16,20},{20,16},{24,28},{28,24},{1,5},{5... | collective-permute-start | bytes 1572872 | tf_op jit(solution)/shard_map/ppermute | solution.py:388
  85.0 1.2 collective-permute-start.21
  85.0 18.1 %collective-permute-start.18 = (s16[1616,128]{1,0:T(8,128)(2,1)S(1)}, s16[1616,128]{1,0:T(8,128)(2,1)S(1)}, u32[]{:S(2)}, u32[]{:S(2)}) collective-permute-start(s16[1616,128]{1,0:T(8,128)(2,1)S(1)} %get-tuple-element.38.rest_1_), channel_id=1, source_target_pairs={{0,8},{4,12},{8,24},{12,28},{16,0},{20,4},{24,16},{28,20},{1,9},{5... | collective-permute-start | bytes 1241096 | tf_op jit(solution)/shard_map/ppermute | solution.py:417
  85.1 30.6 %collective-permute-start.17 = (bf16[128,4096]{1,0:T(8,128)(2,1)S(1)}, bf16[128,4096]{1,0:T(8,128)(2,1)S(1)}, u32[]{:S(2)}, u32[]{:S(2)}) collective-permute-start(bf16[128,4096]{1,0:T(8,128)(2,1)S(1)} %get-tuple-element.37), channel_id=1, source_target_pairs={{0,4},{4,0},{8,12},{12,8},{16,20},{20,16},{24,28},{28,24},{1,5},{5... | collective-permute-start | bytes 3145736 | tf_op jit(solution)/shard_map/ppermute | solution.py:388
  95.8 7.4 %collective-permute-start.22 = (f32[8,128]{1,0:T(8,128)S(1)}, f32[8,128]{1,0:T(8,128)S(1)}, u32[]{:S(2)}, u32[]{:S(2)}) collective-permute-start(f32[8,128]{1,0:T(8,128)S(1)} %get-tuple-element.42), channel_id=1, source_target_pairs={{0,1},{1,0},{2,3},{3,2},{4,5},{5,4},{6,7},{7,6},{8,9},{9,8},{10,11... | collective-permute-start | bytes 12296 | tf_op jit(solution)/shard_map/ppermute | solution.py:421
  95.8 12.6 %collective-permute-start.24 = (s16[1616,128]{1,0:T(8,128)(2,1)S(1)}, s16[1616,128]{1,0:T(8,128)(2,1)S(1)}, u32[]{:S(2)}, u32[]{:S(2)}) collective-permute-start(s16[1616,128]{1,0:T(8,128)(2,1)S(1)} %get-tuple-element.41.rest_1_), channel_id=1, source_target_pairs={{8,16},{12,20},{16,8},{20,12},{9,17},{13,21},{17,9},{21,13},{10,18... | collective-permute-start | bytes 1241096 | tf_op jit(solution)/shard_map/ppermute | solution.py:417
  96.5 16.5 %collective-permute-start.23 = (s16[1616,128]{1,0:T(8,128)(2,1)S(1)}, s16[1616,128]{1,0:T(8,128)(2,1)S(1)}, u32[]{:S(2)}, u32[]{:S(2)}) collective-permute-start(s16[1616,128]{1,0:T(8,128)(2,1)S(1)} %get-tuple-element.41.rest_1_), channel_id=1, source_target_pairs={{0,8},{4,12},{24,16},{28,20},{1,9},{5,13},{25,17},{29,21},{2,10},{... | collective-permute-start | bytes 1241096 | tf_op jit(solution)/shard_map/ppermute | solution.py:417
  105.2 19.7 %collective-permute-start.26 = (s16[1616,128]{1,0:T(8,128)(2,1)S(1)}, s16[1616,128]{1,0:T(8,128)(2,1)S(1)}, u32[]{:S(2)}, u32[]{:S(2)}) collective-permute-start(s16[1616,128]{1,0:T(8,128)(2,1)S(1)} %sum_step_09.1.rest_1_), channel_id=1, source_target_pairs={{8,16},{12,20},{16,8},{20,12},{9,17},{13,21},{17,9},{21,13},{10,18... | collective-permute-start | bytes 1241096 | tf_op jit(solution)/shard_map/ppermute | solution.py:417
  105.9 19.0 %collective-permute-start.25 = (s16[1616,128]{1,0:T(8,128)(2,1)S(1)}, s16[1616,128]{1,0:T(8,128)(2,1)S(1)}, u32[]{:S(2)}, u32[]{:S(2)}) collective-permute-start(s16[1616,128]{1,0:T(8,128)(2,1)S(1)} %sum_step_09.1.rest_1_), channel_id=1, source_target_pairs={{0,8},{4,12},{24,16},{28,20},{1,9},{5,13},{25,17},{29,21},{2,10},{... | collective-permute-start | bytes 1241096 | tf_op jit(solution)/shard_map/ppermute | solution.py:417
  117.7 7.2 %collective-permute-start.27 = (f32[8,128]{1,0:T(8,128)S(1)}, f32[8,128]{1,0:T(8,128)S(1)}, u32[]{:S(2)}, u32[]{:S(2)}) collective-permute-start(f32[8,128]{1,0:T(8,128)S(1)} %get-tuple-element.44), channel_id=1, source_target_pairs={{0,1},{1,0},{2,3},{3,2},{4,5},{5,4},{6,7},{7,6},{8,9},{9,8},{10,11... | collective-permute-start | bytes 12296 | tf_op jit(solution)/shard_map/ppermute | solution.py:421
  117.7 20.0 %collective-permute-start.31 = (s16[1616,128]{1,0:T(8,128)(2,1)S(1)}, s16[1616,128]{1,0:T(8,128)(2,1)S(1)}, u32[]{:S(2)}, u32[]{:S(2)}) collective-permute-start(s16[1616,128]{1,0:T(8,128)(2,1)S(1)} %get-tuple-element.43.rest_1_), channel_id=1, source_target_pairs={{8,16},{12,20},{16,8},{20,12},{9,17},{13,21},{17,9},{21,13},{10,18... | collective-permute-start | bytes 1241096 | tf_op jit(solution)/shard_map/ppermute | solution.py:417
  118.4 19.3 %collective-permute-start.30 = (s16[1616,128]{1,0:T(8,128)(2,1)S(1)}, s16[1616,128]{1,0:T(8,128)(2,1)S(1)}, u32[]{:S(2)}, u32[]{:S(2)}) collective-permute-start(s16[1616,128]{1,0:T(8,128)(2,1)S(1)} %get-tuple-element.43.rest_1_), channel_id=1, source_target_pairs={{0,8},{4,12},{24,16},{28,20},{1,9},{5,13},{25,17},{29,21},{2,10},{... | collective-permute-start | bytes 1241096 | tf_op jit(solution)/shard_map/ppermute | solution.py:417
  126.9 14.6 %collective-permute-start.29 = (s16[1616,128]{1,0:T(8,128)(2,1)S(1)}, s16[1616,128]{1,0:T(8,128)(2,1)S(1)}, u32[]{:S(2)}, u32[]{:S(2)}) collective-permute-start(s16[1616,128]{1,0:T(8,128)(2,1)S(1)} %sum_step_11.1), channel_id=1, source_target_pairs={{8,16},{12,20},{16,8},{20,12},{9,17},{13,21},{17,9},{21,13},{10,18... | collective-permute-start | bytes 1241096 | tf_op jit(solution)/shard_map/ppermute | solution.py:417
  127.6 15.3 %collective-permute-start.28 = (s16[1616,128]{1,0:T(8,128)(2,1)S(1)}, s16[1616,128]{1,0:T(8,128)(2,1)S(1)}, u32[]{:S(2)}, u32[]{:S(2)}) collective-permute-start(s16[1616,128]{1,0:T(8,128)(2,1)S(1)} %sum_step_11.1), channel_id=1, source_target_pairs={{0,8},{4,12},{24,16},{28,20},{1,9},{5,13},{25,17},{29,21},{2,10},{... | collective-permute-start | bytes 1241096 | tf_op jit(solution)/shard_map/ppermute | solution.py:417
where the time goes:
time: 147 us
  waiting for transfers between devices  50.9 us (35%)
  Pallas kernels  50 us (34%)
  starting transfers between devices  39.3 us (27%)
  local copies, waits for them, and re-layouts  3.74 us (3%)
  between operations  1.58 us (1%)
    ppermute x16, waiting for transfers between devices, solve_by_sums(): lax.ppermute(coded, 'ifg', line_permutation(links))  34.9 us
    ppermute x16, starting transfers between devices, solve_by_sums(): lax.ppermute(coded, 'ifg', line_permutation(links))  27.1 us
    pallas_call x12, Pallas kernels, step(): pl.pallas_call(functools.partial(step_kernel, at, layout, earlier is not...  25.1 us
    pallas_call x4, Pallas kernels, finish(): pl.pallas_call(functools.partial(finish_kernel, at, layout, tiles, len(ea...  15 us
    ppermute x8, waiting for transfers between devices, swapped(): here = lax.ppermute(away, 'ifg', swap)  12.7 us
    pallas_call x1, Pallas kernels, invert_classes(): pl.pallas_call(inverse_kernel, out_shape=jax.ShapeDtypeStruct(shape, F32)...  6.77 us
    ppermute x8, starting transfers between devices, swapped(): here = lax.ppermute(away, 'ifg', swap)  6.6 us
    ppermute x1, starting transfers between devices, solve_by_sums(): lax.ppermute(run_counts, 'ifg', line_permutation([(i, line - 1 - i) for i...  5.11 us
  transfers between devices with their start and end apart: 32, of which 13 were waited for; matrix products, arithmetic and copies ran while one was open for 2% of the time, Pallas kernels for 32%

commit v1 on v0

--- a/solution.py
+++ b/solution.py
@@ -22,23 +22,23 @@
 HALVES = 2
 FLIGHT = 2
 FIRST_SWAPS = ((0, 1), (1, 1), (2, 2))
-SWAPS = {2: (4, 2), 3: (6, 2), 5: (8, 2), 6: (10, 2), 7: (12, 4)}
-SWAP_WAITS = {5: 7, 7: 9, 8: 11, 10: 12}
-MEETINGS = (1, 3, 5, 7, 8, 10)
+SWAPS = {2: (4, 2), 3: (6, 2), 5: (8, 4), 8: (12, 4)}
+SWAP_WAITS = {5: 6}
+MEETINGS = ()
 INVERSE_STEP = 2
+FINISHED_AHEAD = 1
 ME, PARTNER, INNER, FIXED = 0, 1, 2, 3
-LATE = 2
 LANES = 128
 CODE_ROWS = 16
 LEVELS = 32700.0
 ROUNDER = 1.5 * 2.0**23
 CODES_PER_OCTAVE = 128.0
 SMALLEST = 2.0**-110
-CHUNK_ORDER = ((3, 2, 1, 0), (0, 3, 2, 1), (3, 0, 1, 2), (0, 1, 2, 3))
+CHUNK_ORDER = ((2, 3, 1, 0), (0, 2, 3, 1), (3, 1, 0, 2), (1, 0, 2, 3))
 SENDS = (
     (((0, 1), (1, 0), (2, 3), (3, 2)),),
+    (((0, 1), (3, 2)), ((1, 2), (2, 1))),
     (((0, 1), (1, 3), (2, 0), (3, 2)),),
-    (((0, 1), (3, 2)), ((1, 2), (2, 1))),
 )
 
 
@@ -301,28 +301,29 @@
         sums_ref[...] += parts[0][0] * scale
 
 
-def finish_kernel(at, layout, tiles, early, table, counts, pairs_ref, own_ref, partner_ref, inverse_ref, *rest):
+def finish_kernel(at, layout, tiles, table, counts, pairs_ref, own_ref, partner_ref, inverse_ref, *rest):
+    first, middle, last = rest[:2], rest[2:4], rest[4:6]
     out_ref, sums_ref = rest[-2:]
     sums_ref[...] = pair_sums(piece_count(at, layout, table, counts), table, pairs_ref, own_ref, partner_ref)
 
     @pl.when(table[INNER] == 0)
     def _():
-        add_arrived(sums_ref, rest[: 2 * early], tiles)
+        add_arrived(sums_ref, first, tiles)
 
     @pl.when(table[INNER] == 1)
     def _():
-        add_arrived(sums_ref, rest[2 * early : 2 * early + 2 * LATE], tiles)
-
+        add_arrived(sums_ref, middle, tiles)
+
+    add_arrived(sums_ref, last, tiles)
     out_ref[...] = split_product(inverse_ref[0, :M, :M], sums_ref[...])
 
 
-def finish(at, part, layout, scalars, pairs, phases, partner, inverse, early, late, series, pixels, piece):
+def finish(at, part, layout, scalars, pairs, phases, partner, inverse, arrived, series, pixels, piece):
     partner, place_in = partner
     local_pairs = phases.shape[0]
     blocks = layout[1]
     tiles = HALVES
     tile = piece // tiles
-    arrived = early + late
     in_specs = [
         pl.BlockSpec(pairs.shape, lambda i, t, c: (0, 0)),
         pl.BlockSpec((local_pairs, tile), lambda i, t, c: (0, t[blocks + at] * tiles + i)),
@@ -336,7 +337,7 @@
         aliases = {len(operands): 0}
         operands.append(series)
     return pl.pallas_call(
-        functools.partial(finish_kernel, at, layout, tiles, len(early)),
+        functools.partial(finish_kernel, at, layout, tiles),
         out_shape=jax.ShapeDtypeStruct((M, pixels), F32),
         grid_spec=pltpu.PrefetchScalarGridSpec(
             num_scalar_prefetch=2,
@@ -392,7 +393,7 @@
     run_counts = counts_of()
     mirrored = lax.ppermute(run_counts, "ifg", line_permutation([(i, line - 1 - i) for i in range(line)]))
     first, count = FIRST_SWAPS[0]
-    chunk, _ = lax.optimization_barrier((jnp.where(place % 2 == 0, line - 1, 0), run_counts))
+    chunk, _ = lax.optimization_barrier((jnp.where(place < line // 2, 2 - 2 * place, 7 - 2 * place), run_counts))
     away = lax.dynamic_slice(phases, (0, ((chunk * 2 + 1 - side) * parts + first) * piece), (local_pairs, piece * count))
     swapped(away, first, count)
     both = jnp.concatenate([run_counts, mirrored])
@@ -401,7 +402,13 @@
     pairs = jnp.concatenate([lax.dynamic_slice(date_pairs, (0, row[at] * local_pairs), (2, local_pairs)) for at in (ME, PARTNER)], axis=1)
     scalars = (row, counts)
 
-    received, coded = [], None
+    received, coded, series = [], None, None
+
+    def finished(part, series):
+        at = steps + part
+        arrived = [received[place * parts + part][-1] for place in range(line - 1)]
+        return finish(at, part, layout, scalars, pairs, phases, partner_of[at], inverse, arrived, series, owner_pixels, piece)
+
     for at in range(steps):
         earlier = received[at - parts][0] if at >= parts else None
         after = [coded] if at else []
@@ -413,6 +420,10 @@
         if at == INVERSE_STEP:
             inverse = invert_classes(date_pairs, run_counts, [coded])
             after.append(inverse)
+        if at == steps - 1:
+            for part in range(FINISHED_AHEAD):
+                series = finished(part, series)
+                after.append(series)
         coded, away, told = step(at, SWAPS.get(at), layout, scalars, pairs, phases, partner_of[at], earlier, after, piece)
         received.append([lax.ppermute(coded, "ifg", line_permutation(links)) for links in SENDS[at // parts]])
         if at in SWAPS:
@@ -422,12 +433,8 @@
         if at == 0:
             swapped(give_out(FIRST_SWAPS[2], layout, row, phases, coded, piece), *FIRST_SWAPS[2])
 
-    series = None
-    for part in range(parts):
-        at = steps + part
-        early = [each for place in range(line - 2) for each in received[place * parts + part]]
-        late = received[(line - 2) * parts + part]
-        series = finish(at, part, layout, scalars, pairs, phases, partner_of[at], inverse, early, late, series, owner_pixels, piece)
+    for part in range(FINISHED_AHEAD, parts):
+        series = finished(part, series)
     return series
 
 

time: 147 us -> 132 us (0.90)
  waiting for transfers between devices: 50.9 us -> 24.3 us
  starting transfers between devices: 39.3 us -> 47.8 us
  local copies, waits for them, and re-layouts: 3.74 us -> 5.65 us
    ppermute x16, waiting for transfers between devices: 34.9 us -> 17.1 us  [solve_by_sums(): lax.ppermute(coded, 'ifg', line_permutation(links))]
    ppermute x16, starting transfers between devices: 27.1 us -> 34.6 us  [solve_by_sums(): lax.ppermute(coded, 'ifg', line_permutation(links))]
    ppermute x8 -> x7, waiting for transfers between devices: 12.7 us -> 5.76 us  [swapped(): here = lax.ppermute(away, 'ifg', swap)]
    ppermute x6 -> x0, waiting for transfers between devices: 1.96 us -> none  [solve_by_sums(): lax.ppermute(told, 'grp', [(i, i ^ 1) for i in range(lax.axis_size('grp'))])]
    unnamed x4 -> x6, local copies, waits for them, and re-layouts: 0.69 us -> 2.61 us
    ppermute x8 -> x7, starting transfers between devices: 6.6 us -> 8.13 us  [swapped(): here = lax.ppermute(away, 'ifg', swap)]
  transfers between devices with their start and end apart: 32 -> 25, of which waited for: 13 -> 10; matrix products, arithmetic and copies ran while one was open for 2% -> 2% of each run, Pallas kernels for 32% -> 36%
where the time goes in v1:
time: 132 us; the launch traced here: 130 us
  Pallas kernels  50 us (38%)
  starting transfers between devices  47.8 us (36%)
  waiting for transfers between devices  24.3 us (18%)
  local copies, waits for them, and re-layouts  5.65 us (4%)
  between operations  1.49 us (1%)
    ppermute x16, starting transfers between devices, solve_by_sums(): lax.ppermute(coded, 'ifg', line_permutation(links))  34.6 us
    pallas_call x12, Pallas kernels, step(): pl.pallas_call(functools.partial(step_kernel, at, layout, earlier is not...  25.1 us
    ppermute x16, waiting for transfers between devices, solve_by_sums(): lax.ppermute(coded, 'ifg', line_permutation(links))  17.1 us
    pallas_call x4, Pallas kernels, finish(): pl.pallas_call(functools.partial(finish_kernel, at, layout, tiles), out_s...  14.2 us
    ppermute x7, starting transfers between devices, swapped(): here = lax.ppermute(away, 'ifg', swap)  8.13 us
    pallas_call x1, Pallas kernels, invert_classes(): pl.pallas_call(inverse_kernel, out_shape=jax.ShapeDtypeStruct(shape, F32)...  7.56 us
    ppermute x7, waiting for transfers between devices, swapped(): here = lax.ppermute(away, 'ifg', swap)  5.76 us
    ppermute x1, starting transfers between devices, solve_by_sums(): lax.ppermute(run_counts, 'ifg', line_permutation([(i, line - 1 - i) for i...  5.11 us
  transfers between devices with their start and end apart: 25, of which 10 were waited for; matrix products, arithmetic and copies ran while one was open for 2% of the time, Pallas kernels for 36%

profile of v1, /device:TPU:0, one launch (start us, length us, event | category | flops | bytes accessed | tf_op | source)
XLA Modules:
  0.0 130.3 jit_solution(990323410200627190)
XLA Ops:
  0.8 0.8 fusion.counts_ref
  1.6 5.1 %collective-permute-start = (s32[2]{0:T(128)S(1)}, s32[2]{0:T(128)S(1)}, u32[]{:S(2)}, u32[]{:S(2)}) collective-permute-start(s32[2]{0:T(128)S(1)} %fusion.counts_ref), channel_id=1, source_target_pairs={{0,24},{4,28},{8,16},{12,20},{16,8},{20,12},{24,0},{28,4},{1,25},{... | collective-permute-start | bytes 32 | tf_op jit(solution)/shard_map/ppermute | solution.py:394
  6.7 1.0 dynamic-slice_bitcast_fusion
  7.7 1.6 %collective-permute-start.2 = (bf16[128,1024]{1,0:T(8,128)(2,1)S(1)}, bf16[128,1024]{1,0:T(8,128)(2,1)S(1)}, u32[]{:S(2)}, u32[]{:S(2)}) collective-permute-start(bf16[128,1024]{1,0:T(8,128)(2,1)S(1)} %dynamic-slice_bitcast_fusion), channel_id=1, source_target_pairs={{0,4},{4,0},{8,12},{12,8},{16,20},{20,16},{24,28},{28,24},{1,5},{5... | collective-permute-start | bytes 786440 | tf_op jit(solution)/shard_map/ppermute | solution.py:389
  11.8 0.7 constant_dynamic-slice_fusion.1
  12.6 1.5 %give_out.3 = bf16[128,1024]{1,0:T(8,128)(2,1)S(1)} custom-call(s32[51]{0:T(128)S(1)} %get-tuple-element.26.table, bf16[128,32768]{1,0:T(8,128)(2,1)} %bitcast.10, s32[2]{0:T(128)S(1)} %collective-permute-done._), custom_call_target="tpu_custom_call" | custom-call | flops 1024 | bytes 1024 | tf_op jit(solution)/shard_map/give_out/pallas_call | solution.py:199
  14.7 1.4 %collective-permute-done.1 = s32[4]{0:T(128)S(1)} collective-permute-done((s32[4]{0:T(128)S(1)}, s32[4]{0:T(128)S(1)}, u32[]{:S(2)}, u32[]{:S(2)}) %collective-permute-start.1) | collective-permute-done | bytes 48 | tf_op jit(solution)/shard_map/ppermute | solution.py:400
  16.2 2.0 %sum_step_00.1._.rest_0_ = s16[1616,128]{1,0:T(8,128)(2,1)S(1)} custom-call(s32[51]{0:T(128)S(1)} %get-tuple-element.26.table, s32[8]{0:T(128)S(1)} %pad_add_fusion.2.counts, s32[2,256]{1,0:T(2,128)S(1)} %pad_add_fusion.pairs_ref, bf16[128,32768]{1,0:T(8,128)(2,1)} %bitcast.11, bf16[128,1024]{1,0:T(8,128)(2,1)S(1)} %collective-permute-done.2.partner_ref), custom_call_target="tpu_custom_call" | custom-call | flops 10000000000 | bytes 30000000 | tf_op jit(solution)/shard_map/sum_step_00/pallas_call | solution.py:271
  18.8 1.6 %give_out.2 = bf16[128,2048]{1,0:T(8,128)(2,1)S(1)} custom-call(s32[51]{0:T(128)S(1)} %get-tuple-element.26.table, bf16[128,32768]{1,0:T(8,128)(2,1)} %bitcast.12, s16[1616,128]{1,0:T(8,128)(2,1)S(1)} %sum_step_00.1._.rest_0_), custom_call_target="tpu_custom_call" | custom-call | flops 1024 | bytes 1024 | tf_op jit(solution)/shard_map/give_out/pallas_call | solution.py:199
  20.4 1.6 %collective-permute-start.3 = (bf16[128,2048]{1,0:T(8,128)(2,1)S(1)}, bf16[128,2048]{1,0:T(8,128)(2,1)S(1)}, u32[]{:S(2)}, u32[]{:S(2)}) collective-permute-start(bf16[128,2048]{1,0:T(8,128)(2,1)S(1)} %give_out.2), channel_id=1, source_target_pairs={{0,4},{4,0},{8,12},{12,8},{16,20},{20,16},{24,28},{28,24},{1,5},{5... | collective-permute-start | bytes 1572872 | tf_op jit(solution)/shard_map/ppermute | solution.py:389
  22.0 2.0 %sum_step_01.1.rest_0_.rest_1_ = s16[1616,128]{1,0:T(8,128)(2,1)S(1)} custom-call(s32[51]{0:T(128)S(1)} %get-tuple-element.26.table, s32[8]{0:T(128)S(1)} %pad_add_fusion.2.counts, s32[2,256]{1,0:T(2,128)S(1)} %pad_add_fusion.pairs_ref, bf16[128,32768]{1,0:T(8,128)(2,1)} %bitcast.13, bf16[128,1024]{1,0:T(8,128)(2,1)S(1)} %collective-permute-done.4.partner_ref, ...), custom_call_target="tpu_custom_call" | custom-call | flops 10000000000 | bytes 30000000 | tf_op jit(solution)/shard_map/sum_step_01/pallas_call | solution.py:271
  24.0 2.0 %collective-permute-start.7 = (s16[1616,128]{1,0:T(8,128)(2,1)S(1)}, s16[1616,128]{1,0:T(8,128)(2,1)S(1)}, u32[]{:S(2)}, u32[]{:S(2)}) collective-permute-start(s16[1616,128]{1,0:T(8,128)(2,1)S(1)} %sum_step_01.1.rest_0_.rest_1_), channel_id=1, source_target_pairs={{0,8},{4,12},{8,0},{12,4},{16,24},{20,28},{24,16},{28,20},{1,9},{5... | collective-permute-start | bytes 1241096 | tf_op jit(solution)/shard_map/ppermute | solution.py:428
  26.0 7.6 %invert_classes_0.1.rest_3_.inverse_ref = f32[2,256,256]{2,1,0:T(8,128)S(1)} custom-call(s32[2]{0:T(128)S(1)} %fusion.counts_ref, s32[2,1024]{1,0:T(2,128)S(1)} %copy-done.2, s16[1616,128]{1,0:T(8,128)(2,1)S(1)} %sum_step_01.1.rest_0_.rest_1_), custom_call_target="tpu_custom_call" | custom-call | flops 1024 | bytes 1024 | tf_op jit(solution)/shard_map/invert_classes_0/pallas_call | solution.py:103
  33.6 2.2 %sum_step_02.1 = (s16[1616,128]{1,0:T(8,128)(2,1)S(1)}, bf16[128,2048]{1,0:T(8,128)(2,1)S(1)}) custom-call(s32[51]{0:T(128)S(1)} %get-tuple-element.26.table, s32[8]{0:T(128)S(1)} %pad_add_fusion.2.counts, s32[2,256]{1,0:T(2,128)S(1)} %pad_add_fusion.pairs_ref, bf16[128,32768]{1,0:T(8,128)(2,1)} %bitcast.14, ...), custom_call_target="tpu_custom_call" | custom-call | flops 10000000000 | bytes 30000000 | tf_op jit(solution)/shard_map/sum_step_02/pallas_call | solution.py:271
  35.8 1.0 collective-permute-start.8
  37.4 0.9 collective-permute-done.7.rest_2_.rest_1_.rest_0_
  38.2 2.2 %sum_step_03.1 = (s16[1616,128]{1,0:T(8,128)(2,1)S(1)}, bf16[128,2048]{1,0:T(8,128)(2,1)S(1)}) custom-call(s32[51]{0:T(128)S(1)} %get-tuple-element.26.table, s32[8]{0:T(128)S(1)} %pad_add_fusion.2.counts, s32[2,256]{1,0:T(2,128)S(1)} %pad_add_fusion.pairs_ref, bf16[128,32768]{1,0:T(8,128)(2,1)} %bitcast.16, ...), custom_call_target="tpu_custom_call" | custom-call | flops 10000000000 | bytes 30000000 | tf_op jit(solution)/shard_map/sum_step_03/pallas_call | solution.py:271
  40.8 2.9 %collective-permute-start.10 = (bf16[128,2048]{1,0:T(8,128)(2,1)S(1)}, bf16[128,2048]{1,0:T(8,128)(2,1)S(1)}, u32[]{:S(2)}, u32[]{:S(2)}) collective-permute-start(bf16[128,2048]{1,0:T(8,128)(2,1)S(1)} %get-tuple-element.18), channel_id=1, source_target_pairs={{0,4},{4,0},{8,12},{12,8},{16,20},{20,16},{24,28},{28,24},{1,5},{5... | collective-permute-start | bytes 1572872 | tf_op jit(solution)/shard_map/ppermute | solution.py:389
  43.7 4.6 %collective-permute-done.8.rest_2_.rest_0_.rest_1_ = s16[1616,128]{1,0:T(8,128)(2,1)S(1)} collective-permute-done((s16[1616,128]{1,0:T(8,128)(2,1)S(1)}, s16[1616,128]{1,0:T(8,128)(2,1)S(1)}, u32[]{:S(2)}, u32[]{:S(2)}) %collective-permute-start.8) | collective-permute-done | bytes 413728 | tf_op jit(solution)/shard_map/ppermute | solution.py:428
  48.3 3.3 %collective-permute-done.6.partner_ref = bf16[128,2048]{1,0:T(8,128)(2,1)S(1)} collective-permute-done((bf16[128,2048]{1,0:T(8,128)(2,1)S(1)}, bf16[128,2048]{1,0:T(8,128)(2,1)S(1)}, u32[]{:S(2)}, u32[]{:S(2)}) %collective-permute-start.6) | collective-permute-done | bytes 524320 | tf_op jit(solution)/shard_map/ppermute | solution.py:389
  51.7 2.0 %sum_step_04.1.rest_2_ = s16[1616,128]{1,0:T(8,128)(2,1)S(1)} custom-call(s32[51]{0:T(128)S(1)} %get-tuple-element.26.table, s32[8]{0:T(128)S(1)} %pad_add_fusion.2.counts, s32[2,256]{1,0:T(2,128)S(1)} %pad_add_fusion.pairs_ref, bf16[128,32768]{1,0:T(8,128)(2,1)} %bitcast.18, bf16[128,2048]{1,0:T(8,128)(2,1)S(1)} %collective-permute-done.6.partner_ref, ...), custom_call_target="tpu_custom_call" | custom-call | flops 10000000000 | bytes 30000000 | tf_op jit(solution)/shard_map/sum_step_04/pallas_call | solution.py:271
  54.4 4.2 %collective-permute-start.12 = (s16[1616,128]{1,0:T(8,128)(2,1)S(1)}, s16[1616,128]{1,0:T(8,128)(2,1)S(1)}, u32[]{:S(2)}, u32[]{:S(2)}) collective-permute-start(s16[1616,128]{1,0:T(8,128)(2,1)S(1)} %sum_step_04.1.rest_2_), channel_id=1, source_target_pairs={{0,8},{4,12},{24,16},{28,20},{1,9},{5,13},{25,17},{29,21},{2,10},{... | collective-permute-start | bytes 1241096 | tf_op jit(solution)/shard_map/ppermute | solution.py:428
  58.6 0.9 collective-permute-done.10.rest_4_.partner_ref
  59.5 2.4 %sum_step_05.1 = (s16[1616,128]{1,0:T(8,128)(2,1)S(1)}, bf16[128,4096]{1,0:T(8,128)(2,1)S(1)}) custom-call(s32[51]{0:T(128)S(1)} %get-tuple-element.26.table, s32[8]{0:T(128)S(1)} %pad_add_fusion.2.counts, s32[2,256]{1,0:T(2,128)S(1)} %pad_add_fusion.pairs_ref, bf16[128,32768]{1,0:T(8,128)(2,1)} %bitcast.20, ...), custom_call_target="tpu_custom_call" | custom-call | flops 10000000000 | bytes 30000000 | tf_op jit(solution)/shard_map/sum_step_05/pallas_call | solution.py:271
  62.7 3.6 %collective-permute-start.14 = (s16[1616,128]{1,0:T(8,128)(2,1)S(1)}, s16[1616,128]{1,0:T(8,128)(2,1)S(1)}, u32[]{:S(2)}, u32[]{:S(2)}) collective-permute-start(s16[1616,128]{1,0:T(8,128)(2,1)S(1)} %get-tuple-element.20.rest_1_), channel_id=1, source_target_pairs={{0,8},{4,12},{24,16},{28,20},{1,9},{5,13},{25,17},{29,21},{2,10},{... | collective-permute-start | bytes 1241096 | tf_op jit(solution)/shard_map/ppermute | solution.py:428
  66.3 0.9 collective-permute-start.11
  67.2 2.0 %sum_step_06.1.rest_1_ = s16[1616,128]{1,0:T(8,128)(2,1)S(1)} custom-call(s32[51]{0:T(128)S(1)} %get-tuple-element.26.table, s32[8]{0:T(128)S(1)} %pad_add_fusion.2.counts, s32[2,256]{1,0:T(2,128)S(1)} %pad_add_fusion.pairs_ref, bf16[128,32768]{1,0:T(8,128)(2,1)} %bitcast.21, bf16[128,2048]{1,0:T(8,128)(2,1)S(1)} %collective-permute-done.10.rest_4_.partner_ref, ...), custom_call_target="tpu_custom_call" | custom-call | flops 10000000000 | bytes 30000000 | tf_op jit(solution)/shard_map/sum_step_06/pallas_call | solution.py:271
  69.9 6.6 %collective-permute-start.16 = (s16[1616,128]{1,0:T(8,128)(2,1)S(1)}, s16[1616,128]{1,0:T(8,128)(2,1)S(1)}, u32[]{:S(2)}, u32[]{:S(2)}) collective-permute-start(s16[1616,128]{1,0:T(8,128)(2,1)S(1)} %sum_step_06.1.rest_1_), channel_id=1, source_target_pairs={{0,8},{4,12},{24,16},{28,20},{1,9},{5,13},{25,17},{29,21},{2,10},{... | collective-permute-start | bytes 1241096 | tf_op jit(solution)/shard_map/ppermute | solution.py:428
  76.5 2.0 %sum_step_07.1.rest_2_ = s16[1616,128]{1,0:T(8,128)(2,1)S(1)} custom-call(s32[51]{0:T(128)S(1)} %get-tuple-element.26.table, s32[8]{0:T(128)S(1)} %pad_add_fusion.2.counts, s32[2,256]{1,0:T(2,128)S(1)} %pad_add_fusion.pairs_ref, bf16[128,32768]{1,0:T(8,128)(2,1)} %bitcast.22, bf16[128,2048]{1,0:T(8,128)(2,1)S(1)} %collective-permute-done.10.rest_4_.partner_ref, ...), custom_call_target="tpu_custom_call" | custom-call | flops 10000000000 | bytes 30000000 | tf_op jit(solution)/shard_map/sum_step_07/pallas_call | solution.py:271
  78.5 3.8 %collective-permute-start.20 = (s16[1616,128]{1,0:T(8,128)(2,1)S(1)}, s16[1616,128]{1,0:T(8,128)(2,1)S(1)}, u32[]{:S(2)}, u32[]{:S(2)}) collective-permute-start(s16[1616,128]{1,0:T(8,128)(2,1)S(1)} %sum_step_07.1.rest_2_), channel_id=1, source_target_pairs={{0,8},{4,12},{24,16},{28,20},{1,9},{5,13},{25,17},{29,21},{2,10},{... | collective-permute-start | bytes 1241096 | tf_op jit(solution)/shard_map/ppermute | solution.py:428
  83.0 3.5 %collective-permute-done.16.rest_3_.rest_0_ = s16[1616,128]{1,0:T(8,128)(2,1)S(1)} collective-permute-done((s16[1616,128]{1,0:T(8,128)(2,1)S(1)}, s16[1616,128]{1,0:T(8,128)(2,1)S(1)}, u32[]{:S(2)}, u32[]{:S(2)}) %collective-permute-start.16) | collective-permute-done | bytes 413728 | tf_op jit(solution)/shard_map/ppermute | solution.py:428
  86.4 0.7 collective-permute-done.11.partner_ref
  87.1 2.4 %sum_step_08.1 = (s16[1616,128]{1,0:T(8,128)(2,1)S(1)}, bf16[128,4096]{1,0:T(8,128)(2,1)S(1)}) custom-call(s32[51]{0:T(128)S(1)} %get-tuple-element.26.table, s32[8]{0:T(128)S(1)} %pad_add_fusion.2.counts, s32[2,256]{1,0:T(2,128)S(1)} %pad_add_fusion.pairs_ref, bf16[128,32768]{1,0:T(8,128)(2,1)} %bitcast.23, ...), custom_call_target="tpu_custom_call" | custom-call | flops 10000000000 | bytes 30000000 | tf_op jit(solution)/shard_map/sum_step_08/pallas_call | solution.py:271
  89.6 1.8 %collective-permute-start.21 = (s16[1616,128]{1,0:T(8,128)(2,1)S(1)}, s16[1616,128]{1,0:T(8,128)(2,1)S(1)}, u32[]{:S(2)}, u32[]{:S(2)}) collective-permute-start(s16[1616,128]{1,0:T(8,128)(2,1)S(1)} %get-tuple-element.22.rest_1_), channel_id=1, source_target_pairs={{0,8},{4,12},{8,24},{12,28},{16,0},{20,4},{24,16},{28,20},{1,9},{5... | collective-permute-start | bytes 1241096 | tf_op jit(solution)/shard_map/ppermute | solution.py:428
  91.5 3.8 %collective-permute-done.20.rest_2_.rest_0_ = s16[1616,128]{1,0:T(8,128)(2,1)S(1)} collective-permute-done((s16[1616,128]{1,0:T(8,128)(2,1)S(1)}, s16[1616,128]{1,0:T(8,128)(2,1)S(1)}, u32[]{:S(2)}, u32[]{:S(2)}) %collective-permute-start.20) | collective-permute-done | bytes 413728 | tf_op jit(solution)/shard_map/ppermute | solution.py:428
  95.3 2.0 %sum_step_09.1.rest_1_ = s16[1616,128]{1,0:T(8,128)(2,1)S(1)} custom-call(s32[51]{0:T(128)S(1)} %get-tuple-element.26.table, s32[8]{0:T(128)S(1)} %pad_add_fusion.2.counts, s32[2,256]{1,0:T(2,128)S(1)} %pad_add_fusion.pairs_ref, bf16[128,32768]{1,0:T(8,128)(2,1)} %bitcast.25, bf16[128,4096]{1,0:T(8,128)(2,1)S(1)} %collective-permute-done.11.partner_ref, ...), custom_call_target="tpu_custom_call" | custom-call | flops 10000000000 | bytes 30000000 | tf_op jit(solution)/shard_map/sum_step_09/pallas_call | solution.py:271
  97.3 2.5 %collective-permute-start.22 = (s16[1616,128]{1,0:T(8,128)(2,1)S(1)}, s16[1616,128]{1,0:T(8,128)(2,1)S(1)}, u32[]{:S(2)}, u32[]{:S(2)}) collective-permute-start(s16[1616,128]{1,0:T(8,128)(2,1)S(1)} %sum_step_09.1.rest_1_), channel_id=1, source_target_pairs={{0,8},{4,12},{8,24},{12,28},{16,0},{20,4},{24,16},{28,20},{1,9},{5... | collective-permute-start | bytes 1241096 | tf_op jit(solution)/shard_map/ppermute | solution.py:428
  99.8 4.3 %collective-permute-done.21.rest_2_.rest_4_.rest_5_ = s16[1616,128]{1,0:T(8,128)(2,1)S(1)} collective-permute-done((s16[1616,128]{1,0:T(8,128)(2,1)S(1)}, s16[1616,128]{1,0:T(8,128)(2,1)S(1)}, u32[]{:S(2)}, u32[]{:S(2)}) %collective-permute-start.21) | collective-permute-done | bytes 413728 | tf_op jit(solution)/shard_map/ppermute | solution.py:428
  104.2 2.0 %sum_step_10.1.rest_1_ = s16[1616,128]{1,0:T(8,128)(2,1)S(1)} custom-call(s32[51]{0:T(128)S(1)} %get-tuple-element.26.table, s32[8]{0:T(128)S(1)} %pad_add_fusion.2.counts, s32[2,256]{1,0:T(2,128)S(1)} %pad_add_fusion.pairs_ref, bf16[128,32768]{1,0:T(8,128)(2,1)} %bitcast.26, bf16[128,4096]{1,0:T(8,128)(2,1)S(1)} %collective-permute-done.11.partner_ref, ...), custom_call_target="tpu_custom_call" | custom-call | flops 10000000000 | bytes 30000000 | tf_op jit(solution)/shard_map/sum_step_10/pallas_call | solution.py:271
  106.2 2.5 %collective-permute-start.24 = (s16[1616,128]{1,0:T(8,128)(2,1)S(1)}, s16[1616,128]{1,0:T(8,128)(2,1)S(1)}, u32[]{:S(2)}, u32[]{:S(2)}) collective-permute-start(s16[1616,128]{1,0:T(8,128)(2,1)S(1)} %sum_step_10.1.rest_1_), channel_id=1, source_target_pairs={{0,8},{4,12},{8,24},{12,28},{16,0},{20,4},{24,16},{28,20},{1,9},{5... | collective-permute-start | bytes 1241096 | tf_op jit(solution)/shard_map/ppermute | solution.py:428
  108.7 0.8 collective-permute-done.18.partner_ref
  109.5 3.6 %finish_0.1.rest_3_.rest_6_ = f32[200,4096]{1,0:T(8,128)} custom-call(s32[51]{0:T(128)S(1)} %get-tuple-element.26.table, s32[8]{0:T(128)S(1)} %pad_add_fusion.2.counts, s32[2,256]{1,0:T(2,128)S(1)} %pad_add_fusion.pairs_ref, bf16[128,32768]{1,0:T(8,128)(2,1)} %bitcast.27, bf16[128,4096]{1,0:T(8,128)(2,1)S(1)} %collective-permute-done.18.partner_ref, ...), custom_call_target="tpu_custom_call" | custom-call | flops 1024 | bytes 1024 | tf_op jit(solution)/shard_map/finish_0/pallas_call | solution.py:339
  113.1 1.9 %copy-done.1 = f32[200,4096]{1,0:T(8,128)S(1)} copy-done((f32[200,4096]{1,0:T(8,128)S(1)}, f32[200,4096]{1,0:T(8,128)}, u32[]{:S(2)}) %copy-start.1) | copy-done | bytes 3276824
  115.0 2.0 %sum_step_11.1 = s16[1616,128]{1,0:T(8,128)(2,1)S(1)} custom-call(s32[51]{0:T(128)S(1)} %get-tuple-element.26.table, s32[8]{0:T(128)S(1)} %pad_add_fusion.2.counts, s32[2,256]{1,0:T(2,128)S(1)} %pad_add_fusion.pairs_ref, bf16[128,32768]{1,0:T(8,128)(2,1)} %bitcast.28, bf16[128,4096]{1,0:T(8,128)(2,1)S(1)} %collective-permute-done.11.partner_ref, ...), custom_call_target="tpu_custom_call" | custom-call | flops 10000000000 | bytes 30000000 | tf_op jit(solution)/shard_map/sum_step_11/pallas_call | solution.py:271
  117.0 2.6 %collective-permute-start.23 = (s16[1616,128]{1,0:T(8,128)(2,1)S(1)}, s16[1616,128]{1,0:T(8,128)(2,1)S(1)}, u32[]{:S(2)}, u32[]{:S(2)}) collective-permute-start(s16[1616,128]{1,0:T(8,128)(2,1)S(1)} %sum_step_11.1), channel_id=1, source_target_pairs={{0,8},{4,12},{8,24},{12,28},{16,0},{20,4},{24,16},{28,20},{1,9},{5... | collective-permute-start | bytes 1241096 | tf_op jit(solution)/shard_map/ppermute | solution.py:428
  119.6 3.6 %finish_1.1.rest_6_ = f32[200,4096]{1,0:T(8,128)} custom-call(s32[51]{0:T(128)S(1)} %get-tuple-element.26.table, s32[8]{0:T(128)S(1)} %pad_add_fusion.2.counts, s32[2,256]{1,0:T(2,128)S(1)} %pad_add_fusion.pairs_ref, bf16[128,32768]{1,0:T(8,128)(2,1)} %bitcast.29, ...), custom_call_target="tpu_custom_call", output_to_operand_aliasing={{}: (12, {})} | custom-call | flops 1024 | bytes 1024 | tf_op jit(solution)/shard_map/finish_1/pallas_call | solution.py:339
  123.2 3.6 %finish_2.1.rest_6_ = f32[200,4096]{1,0:T(8,128)} custom-call(s32[51]{0:T(128)S(1)} %get-tuple-element.26.table, s32[8]{0:T(128)S(1)} %pad_add_fusion.2.counts, s32[2,256]{1,0:T(2,128)S(1)} %pad_add_fusion.pairs_ref, bf16[128,32768]{1,0:T(8,128)(2,1)} %bitcast.30, ...), custom_call_target="tpu_custom_call", output_to_operand_aliasing={{}: (12, {})} | custom-call | flops 1024 | bytes 1024 | tf_op jit(solution)/shard_map/finish_2/pallas_call | solution.py:339
  126.7 3.6 %finish_3.1 = f32[200,4096]{1,0:T(8,128)} custom-call(s32[51]{0:T(128)S(1)} %get-tuple-element.26.table, s32[8]{0:T(128)S(1)} %pad_add_fusion.2.counts, s32[2,256]{1,0:T(2,128)S(1)} %pad_add_fusion.pairs_ref, bf16[128,32768]{1,0:T(8,128)(2,1)} %bitcast.31, ...), custom_call_target="tpu_custom_call", output_to_operand_aliasing={{}: (12, {})} | custom-call | flops 1024 | bytes 1024 | tf_op jit(solution)/shard_map/finish_3/pallas_call | solution.py:339
  (37 shorter events, 7.3 us)
Async XLA Ops:
  0.0 0.7 copy-start
  1.6 10.8 %collective-permute-start = (s32[2]{0:T(128)S(1)}, s32[2]{0:T(128)S(1)}, u32[]{:S(2)}, u32[]{:S(2)}) collective-permute-start(s32[2]{0:T(128)S(1)} %fusion.counts_ref), channel_id=1, source_target_pairs={{0,24},{4,28},{8,16},{12,20},{16,8},{20,12},{24,0},{28,4},{1,25},{... | collective-permute-start | bytes 32 | tf_op jit(solution)/shard_map/ppermute | solution.py:394
  7.7 8.5 %collective-permute-start.2 = (bf16[128,1024]{1,0:T(8,128)(2,1)S(1)}, bf16[128,1024]{1,0:T(8,128)(2,1)S(1)}, u32[]{:S(2)}, u32[]{:S(2)}) collective-permute-start(bf16[128,1024]{1,0:T(8,128)(2,1)S(1)} %dynamic-slice_bitcast_fusion), channel_id=1, source_target_pairs={{0,4},{4,0},{8,12},{12,8},{16,20},{20,16},{24,28},{28,24},{1,5},{5... | collective-permute-start | bytes 786440 | tf_op jit(solution)/shard_map/ppermute | solution.py:389
  12.5 3.5 %collective-permute-start.1 = (s32[4]{0:T(128)S(1)}, s32[4]{0:T(128)S(1)}, u32[]{:S(2)}, u32[]{:S(2)}) collective-permute-start(s32[4]{0:T(128)S(1)} %pad_add_fusion.1), channel_id=1, source_target_pairs={{0,8},{4,12},{8,0},{12,4},{16,24},{20,28},{24,16},{28,20},{1,9},{5... | collective-permute-start | bytes 56 | tf_op jit(solution)/shard_map/ppermute | solution.py:400
  14.1 7.9 %collective-permute-start.4 = (bf16[128,1024]{1,0:T(8,128)(2,1)S(1)}, bf16[128,1024]{1,0:T(8,128)(2,1)S(1)}, u32[]{:S(2)}, u32[]{:S(2)}) collective-permute-start(bf16[128,1024]{1,0:T(8,128)(2,1)S(1)} %give_out.3), channel_id=1, source_target_pairs={{0,4},{4,0},{8,12},{12,8},{16,20},{20,16},{24,28},{28,24},{1,5},{5... | collective-permute-start | bytes 786440 | tf_op jit(solution)/shard_map/ppermute | solution.py:389
  18.1 15.5 %collective-permute-start.5 = (s16[1616,128]{1,0:T(8,128)(2,1)S(1)}, s16[1616,128]{1,0:T(8,128)(2,1)S(1)}, u32[]{:S(2)}, u32[]{:S(2)}) collective-permute-start(s16[1616,128]{1,0:T(8,128)(2,1)S(1)} %sum_step_00.1._.rest_0_), channel_id=1, source_target_pairs={{0,8},{4,12},{8,0},{12,4},{16,24},{20,28},{24,16},{28,20},{1,9},{5... | collective-permute-start | bytes 1241096 | tf_op jit(solution)/shard_map/ppermute | solution.py:428
  20.4 5.6 %copy-start.2 = (s32[2,1024]{1,0:T(2,128)S(1)}, s32[2,1024]{1,0:T(2,128)}, u32[]{:S(2)}) copy-start(s32[2,1024]{1,0:T(2,128)} %pairs_ref.1) | copy-start | bytes 24580
  20.4 13.2 %collective-permute-start.3 = (bf16[128,2048]{1,0:T(8,128)(2,1)S(1)}, bf16[128,2048]{1,0:T(8,128)(2,1)S(1)}, u32[]{:S(2)}, u32[]{:S(2)}) collective-permute-start(bf16[128,2048]{1,0:T(8,128)(2,1)S(1)} %give_out.2), channel_id=1, source_target_pairs={{0,4},{4,0},{8,12},{12,8},{16,20},{20,16},{24,28},{28,24},{1,5},{5... | collective-permute-start | bytes 1572872 | tf_op jit(solution)/shard_map/ppermute | solution.py:389
  24.0 14.3 %collective-permute-start.7 = (s16[1616,128]{1,0:T(8,128)(2,1)S(1)}, s16[1616,128]{1,0:T(8,128)(2,1)S(1)}, u32[]{:S(2)}, u32[]{:S(2)}) collective-permute-start(s16[1616,128]{1,0:T(8,128)(2,1)S(1)} %sum_step_01.1.rest_0_.rest_1_), channel_id=1, source_target_pairs={{0,8},{4,12},{8,0},{12,4},{16,24},{20,28},{24,16},{28,20},{1,9},{5... | collective-permute-start | bytes 1241096 | tf_op jit(solution)/shard_map/ppermute | solution.py:428
  35.8 12.6 %collective-permute-start.8 = (s16[1616,128]{1,0:T(8,128)(2,1)S(1)}, s16[1616,128]{1,0:T(8,128)(2,1)S(1)}, u32[]{:S(2)}, u32[]{:S(2)}) collective-permute-start(s16[1616,128]{1,0:T(8,128)(2,1)S(1)} %get-tuple-element.16.rest_1_), channel_id=1, source_target_pairs={{0,8},{4,12},{8,0},{12,4},{16,24},{20,28},{24,16},{28,20},{1,9},{5... | collective-permute-start | bytes 1241096 | tf_op jit(solution)/shard_map/ppermute | solution.py:428
  36.8 14.9 %collective-permute-start.6 = (bf16[128,2048]{1,0:T(8,128)(2,1)S(1)}, bf16[128,2048]{1,0:T(8,128)(2,1)S(1)}, u32[]{:S(2)}, u32[]{:S(2)}) collective-permute-start(bf16[128,2048]{1,0:T(8,128)(2,1)S(1)} %get-tuple-element.15), channel_id=1, source_target_pairs={{0,4},{4,0},{8,12},{12,8},{16,20},{20,16},{24,28},{28,24},{1,5},{5... | collective-permute-start | bytes 1572872 | tf_op jit(solution)/shard_map/ppermute | solution.py:389
  40.4 18.2 %collective-permute-start.9 = (s16[1616,128]{1,0:T(8,128)(2,1)S(1)}, s16[1616,128]{1,0:T(8,128)(2,1)S(1)}, u32[]{:S(2)}, u32[]{:S(2)}) collective-permute-start(s16[1616,128]{1,0:T(8,128)(2,1)S(1)} %get-tuple-element.17.rest_1_), channel_id=1, source_target_pairs={{0,8},{4,12},{8,0},{12,4},{16,24},{20,28},{24,16},{28,20},{1,9},{5... | collective-permute-start | bytes 1241096 | tf_op jit(solution)/shard_map/ppermute | solution.py:428
  40.8 18.8 %collective-permute-start.10 = (bf16[128,2048]{1,0:T(8,128)(2,1)S(1)}, bf16[128,2048]{1,0:T(8,128)(2,1)S(1)}, u32[]{:S(2)}, u32[]{:S(2)}) collective-permute-start(bf16[128,2048]{1,0:T(8,128)(2,1)S(1)} %get-tuple-element.18), channel_id=1, source_target_pairs={{0,4},{4,0},{8,12},{12,8},{16,20},{20,16},{24,28},{28,24},{1,5},{5... | collective-permute-start | bytes 1572872 | tf_op jit(solution)/shard_map/ppermute | solution.py:389
  53.7 13.5 %collective-permute-start.13 = (s16[1616,128]{1,0:T(8,128)(2,1)S(1)}, s16[1616,128]{1,0:T(8,128)(2,1)S(1)}, u32[]{:S(2)}, u32[]{:S(2)}) collective-permute-start(s16[1616,128]{1,0:T(8,128)(2,1)S(1)} %sum_step_04.1.rest_2_), channel_id=1, source_target_pairs={{8,16},{12,20},{16,8},{20,12},{9,17},{13,21},{17,9},{21,13},{10,18... | collective-permute-start | bytes 1241096 | tf_op jit(solution)/shard_map/ppermute | solution.py:428
  54.4 12.8 %collective-permute-start.12 = (s16[1616,128]{1,0:T(8,128)(2,1)S(1)}, s16[1616,128]{1,0:T(8,128)(2,1)S(1)}, u32[]{:S(2)}, u32[]{:S(2)}) collective-permute-start(s16[1616,128]{1,0:T(8,128)(2,1)S(1)} %sum_step_04.1.rest_2_), channel_id=1, source_target_pairs={{0,8},{4,12},{24,16},{28,20},{1,9},{5,13},{25,17},{29,21},{2,10},{... | collective-permute-start | bytes 1241096 | tf_op jit(solution)/shard_map/ppermute | solution.py:428
  62.0 14.5 %collective-permute-start.15 = (s16[1616,128]{1,0:T(8,128)(2,1)S(1)}, s16[1616,128]{1,0:T(8,128)(2,1)S(1)}, u32[]{:S(2)}, u32[]{:S(2)}) collective-permute-start(s16[1616,128]{1,0:T(8,128)(2,1)S(1)} %get-tuple-element.20.rest_1_), channel_id=1, source_target_pairs={{8,16},{12,20},{16,8},{20,12},{9,17},{13,21},{17,9},{21,13},{10,18... | collective-permute-start | bytes 1241096 | tf_op jit(solution)/shard_map/ppermute | solution.py:428
  62.7 13.8 %collective-permute-start.14 = (s16[1616,128]{1,0:T(8,128)(2,1)S(1)}, s16[1616,128]{1,0:T(8,128)(2,1)S(1)}, u32[]{:S(2)}, u32[]{:S(2)}) collective-permute-start(s16[1616,128]{1,0:T(8,128)(2,1)S(1)} %get-tuple-element.20.rest_1_), channel_id=1, source_target_pairs={{0,8},{4,12},{24,16},{28,20},{1,9},{5,13},{25,17},{29,21},{2,10},{... | collective-permute-start | bytes 1241096 | tf_op jit(solution)/shard_map/ppermute | solution.py:428
  66.3 20.8 %collective-permute-start.11 = (bf16[128,4096]{1,0:T(8,128)(2,1)S(1)}, bf16[128,4096]{1,0:T(8,128)(2,1)S(1)}, u32[]{:S(2)}, u32[]{:S(2)}) collective-permute-start(bf16[128,4096]{1,0:T(8,128)(2,1)S(1)} %get-tuple-element.19), channel_id=1, source_target_pairs={{0,4},{4,0},{8,12},{12,8},{16,20},{20,16},{24,28},{28,24},{1,5},{5... | collective-permute-start | bytes 3145736 | tf_op jit(solution)/shard_map/ppermute | solution.py:389
  69.2 13.8 %collective-permute-start.17 = (s16[1616,128]{1,0:T(8,128)(2,1)S(1)}, s16[1616,128]{1,0:T(8,128)(2,1)S(1)}, u32[]{:S(2)}, u32[]{:S(2)}) collective-permute-start(s16[1616,128]{1,0:T(8,128)(2,1)S(1)} %sum_step_06.1.rest_1_), channel_id=1, source_target_pairs={{8,16},{12,20},{16,8},{20,12},{9,17},{13,21},{17,9},{21,13},{10,18... | collective-permute-start | bytes 1241096 | tf_op jit(solution)/shard_map/ppermute | solution.py:428
  69.9 16.5 %collective-permute-start.16 = (s16[1616,128]{1,0:T(8,128)(2,1)S(1)}, s16[1616,128]{1,0:T(8,128)(2,1)S(1)}, u32[]{:S(2)}, u32[]{:S(2)}) collective-permute-start(s16[1616,128]{1,0:T(8,128)(2,1)S(1)} %sum_step_06.1.rest_1_), channel_id=1, source_target_pairs={{0,8},{4,12},{24,16},{28,20},{1,9},{5,13},{25,17},{29,21},{2,10},{... | collective-permute-start | bytes 1241096 | tf_op jit(solution)/shard_map/ppermute | solution.py:428
  78.5 16.8 %collective-permute-start.20 = (s16[1616,128]{1,0:T(8,128)(2,1)S(1)}, s16[1616,128]{1,0:T(8,128)(2,1)S(1)}, u32[]{:S(2)}, u32[]{:S(2)}) collective-permute-start(s16[1616,128]{1,0:T(8,128)(2,1)S(1)} %sum_step_07.1.rest_2_), channel_id=1, source_target_pairs={{0,8},{4,12},{24,16},{28,20},{1,9},{5,13},{25,17},{29,21},{2,10},{... | collective-permute-start | bytes 1241096 | tf_op jit(solution)/shard_map/ppermute | solution.py:428
  82.3 13.0 %collective-permute-start.19 = (s16[1616,128]{1,0:T(8,128)(2,1)S(1)}, s16[1616,128]{1,0:T(8,128)(2,1)S(1)}, u32[]{:S(2)}, u32[]{:S(2)}) collective-permute-start(s16[1616,128]{1,0:T(8,128)(2,1)S(1)} %sum_step_07.1.rest_2_), channel_id=1, source_target_pairs={{8,16},{12,20},{16,8},{20,12},{9,17},{13,21},{17,9},{21,13},{10,18... | collective-permute-start | bytes 1241096 | tf_op jit(solution)/shard_map/ppermute | solution.py:428
  89.6 14.6 %collective-permute-start.21 = (s16[1616,128]{1,0:T(8,128)(2,1)S(1)}, s16[1616,128]{1,0:T(8,128)(2,1)S(1)}, u32[]{:S(2)}, u32[]{:S(2)}) collective-permute-start(s16[1616,128]{1,0:T(8,128)(2,1)S(1)} %get-tuple-element.22.rest_1_), channel_id=1, source_target_pairs={{0,8},{4,12},{8,24},{12,28},{16,0},{20,4},{24,16},{28,20},{1,9},{5... | collective-permute-start | bytes 1241096 | tf_op jit(solution)/shard_map/ppermute | solution.py:428
  91.4 18.1 %collective-permute-start.18 = (bf16[128,4096]{1,0:T(8,128)(2,1)S(1)}, bf16[128,4096]{1,0:T(8,128)(2,1)S(1)}, u32[]{:S(2)}, u32[]{:S(2)}) collective-permute-start(bf16[128,4096]{1,0:T(8,128)(2,1)S(1)} %get-tuple-element.21), channel_id=1, source_target_pairs={{0,4},{4,0},{8,12},{12,8},{16,20},{20,16},{24,28},{28,24},{1,5},{5... | collective-permute-start | bytes 3145736 | tf_op jit(solution)/shard_map/ppermute | solution.py:389
  97.3 15.8 %collective-permute-start.22 = (s16[1616,128]{1,0:T(8,128)(2,1)S(1)}, s16[1616,128]{1,0:T(8,128)(2,1)S(1)}, u32[]{:S(2)}, u32[]{:S(2)}) collective-permute-start(s16[1616,128]{1,0:T(8,128)(2,1)S(1)} %sum_step_09.1.rest_1_), channel_id=1, source_target_pairs={{0,8},{4,12},{8,24},{12,28},{16,0},{20,4},{24,16},{28,20},{1,9},{5... | collective-permute-start | bytes 1241096 | tf_op jit(solution)/shard_map/ppermute | solution.py:428
  106.2 17.0 %collective-permute-start.24 = (s16[1616,128]{1,0:T(8,128)(2,1)S(1)}, s16[1616,128]{1,0:T(8,128)(2,1)S(1)}, u32[]{:S(2)}, u32[]{:S(2)}) collective-permute-start(s16[1616,128]{1,0:T(8,128)(2,1)S(1)} %sum_step_10.1.rest_1_), channel_id=1, source_target_pairs={{0,8},{4,12},{8,24},{12,28},{16,0},{20,4},{24,16},{28,20},{1,9},{5... | collective-permute-start | bytes 1241096 | tf_op jit(solution)/shard_map/ppermute | solution.py:428
  113.1 1.9 %copy-start.1 = (f32[200,4096]{1,0:T(8,128)S(1)}, f32[200,4096]{1,0:T(8,128)}, u32[]{:S(2)}) copy-start(f32[200,4096]{1,0:T(8,128)} %finish_0.1.rest_3_.rest_6_) | copy-start | bytes 9830404
  117.0 9.7 %collective-permute-start.23 = (s16[1616,128]{1,0:T(8,128)(2,1)S(1)}, s16[1616,128]{1,0:T(8,128)(2,1)S(1)}, u32[]{:S(2)}, u32[]{:S(2)}) collective-permute-start(s16[1616,128]{1,0:T(8,128)(2,1)S(1)} %sum_step_11.1), channel_id=1, source_target_pairs={{0,8},{4,12},{8,24},{12,28},{16,0},{20,4},{24,16},{28,20},{1,9},{5... | collective-permute-start | bytes 1241096 | tf_op jit(solution)/shard_map/ppermute | solution.py:428

commit v2 on v1

--- a/solution.py
+++ b/solution.py
@@ -22,11 +22,11 @@
 HALVES = 2
 FLIGHT = 2
 FIRST_SWAPS = ((0, 1), (1, 1), (2, 2))
-SWAPS = {2: (4, 2), 3: (6, 2), 5: (8, 4), 8: (12, 4)}
-SWAP_WAITS = {5: 6}
+SWAPS = {2: (4, 2), 3: (6, 2), 5: (8, 4), 8: (12, 2), 9: (14, 2)}
+SWAP_WAITS = {5: 6, 10: 12}
 MEETINGS = ()
 INVERSE_STEP = 2
-FINISHED_AHEAD = 1
+FINISHED_AHEAD = 0
 ME, PARTNER, INNER, FIXED = 0, 1, 2, 3
 LANES = 128
 CODE_ROWS = 16

time: 132 us -> 134 us (1.015)
  starting transfers between devices: 47.8 us -> 51.1 us
  local copies, waits for them, and re-layouts: 5.65 us -> 3.8 us
  waiting for transfers between devices: 24.3 us -> 25.7 us
    ppermute x16, waiting for transfers between devices: 17.1 us -> 19.1 us  [solve_by_sums(): lax.ppermute(coded, 'ifg', line_permutation(links))]
    unnamed x6 -> x4, local copies, waits for them, and re-layouts: 2.61 us -> 0.69 us
    ppermute x16, starting transfers between devices: 34.6 us -> 36.2 us  [solve_by_sums(): lax.ppermute(coded, 'ifg', line_permutation(links))]
    ppermute x7 -> x8, starting transfers between devices: 8.13 us -> 9.73 us  [swapped(): here = lax.ppermute(away, 'ifg', swap)]
    ppermute x7 -> x8, waiting for transfers between devices: 5.76 us -> 5.1 us  [swapped(): here = lax.ppermute(away, 'ifg', swap)]
  transfers between devices with their start and end apart: 25 -> 26, of which waited for: 10 -> 9; matrix products, arithmetic and copies ran while one was open for 2% -> 2% of each run, Pallas kernels for 36% -> 35%
where the time goes in v2:
time: 134 us; the launch traced here: 133 us
  starting transfers between devices  51.1 us (38%)
  Pallas kernels  50 us (37%)
  waiting for transfers between devices  25.7 us (19%)
  local copies, waits for them, and re-layouts  3.8 us (3%)
  between operations  1.58 us (1%)
    ppermute x16, starting transfers between devices, solve_by_sums(): lax.ppermute(coded, 'ifg', line_permutation(links))  36.2 us
    pallas_call x12, Pallas kernels, step(): pl.pallas_call(functools.partial(step_kernel, at, layout, earlier is not...  25.1 us
    ppermute x16, waiting for transfers between devices, solve_by_sums(): lax.ppermute(coded, 'ifg', line_permutation(links))  19.1 us
    pallas_call x4, Pallas kernels, finish(): pl.pallas_call(functools.partial(finish_kernel, at, layout, tiles), out_s...  14.2 us
    ppermute x8, starting transfers between devices, swapped(): here = lax.ppermute(away, 'ifg', swap)  9.73 us
    pallas_call x1, Pallas kernels, invert_classes(): pl.pallas_call(inverse_kernel, out_shape=jax.ShapeDtypeStruct(shape, F32)...  7.55 us
    ppermute x1, starting transfers between devices, solve_by_sums(): lax.ppermute(run_counts, 'ifg', line_permutation([(i, line - 1 - i) for i...  5.11 us
    ppermute x8, waiting for transfers between devices, swapped(): here = lax.ppermute(away, 'ifg', swap)  5.1 us
  transfers between devices with their start and end apart: 26, of which 9 were waited for; matrix products, arithmetic and copies ran while one was open for 2% of the time, Pallas kernels for 35%

profile of v2, /device:TPU:0, one launch (start us, length us, event | category | flops | bytes accessed | tf_op | source)
XLA Modules:
  0.0 133.1 jit_solution(13336529246436579282)
XLA Ops:
  0.8 0.8 fusion.counts_ref
  1.6 5.1 %collective-permute-start = (s32[2]{0:T(128)S(1)}, s32[2]{0:T(128)S(1)}, u32[]{:S(2)}, u32[]{:S(2)}) collective-permute-start(s32[2]{0:T(128)S(1)} %fusion.counts_ref), channel_id=1, source_target_pairs={{0,24},{4,28},{8,16},{12,20},{16,8},{20,12},{24,0},{28,4},{1,25},{... | collective-permute-start | bytes 32 | tf_op jit(solution)/shard_map/ppermute | solution.py:394
  6.7 1.0 dynamic-slice_bitcast_fusion
  7.7 1.6 %collective-permute-start.2 = (bf16[128,1024]{1,0:T(8,128)(2,1)S(1)}, bf16[128,1024]{1,0:T(8,128)(2,1)S(1)}, u32[]{:S(2)}, u32[]{:S(2)}) collective-permute-start(bf16[128,1024]{1,0:T(8,128)(2,1)S(1)} %dynamic-slice_bitcast_fusion), channel_id=1, source_target_pairs={{0,4},{4,0},{8,12},{12,8},{16,20},{20,16},{24,28},{28,24},{1,5},{5... | collective-permute-start | bytes 786440 | tf_op jit(solution)/shard_map/ppermute | solution.py:389
  9.3 0.7 constant_dynamic-slice_fusion.3
  11.9 0.7 constant_dynamic-slice_fusion.1
  12.7 1.5 %give_out.3 = bf16[128,1024]{1,0:T(8,128)(2,1)S(1)} custom-call(s32[51]{0:T(128)S(1)} %get-tuple-element.30.table, bf16[128,32768]{1,0:T(8,128)(2,1)} %bitcast.10, s32[2]{0:T(128)S(1)} %collective-permute-done._), custom_call_target="tpu_custom_call" | custom-call | flops 1024 | bytes 1024 | tf_op jit(solution)/shard_map/give_out/pallas_call | solution.py:199
  14.8 1.4 %collective-permute-done.1 = s32[4]{0:T(128)S(1)} collective-permute-done((s32[4]{0:T(128)S(1)}, s32[4]{0:T(128)S(1)}, u32[]{:S(2)}, u32[]{:S(2)}) %collective-permute-start.1) | collective-permute-done | bytes 48 | tf_op jit(solution)/shard_map/ppermute | solution.py:400
  16.3 2.0 %sum_step_00.1._.rest_0_ = s16[1616,128]{1,0:T(8,128)(2,1)S(1)} custom-call(s32[51]{0:T(128)S(1)} %get-tuple-element.30.table, s32[8]{0:T(128)S(1)} %pad_add_fusion.2.counts, s32[2,256]{1,0:T(2,128)S(1)} %pad_add_fusion.pairs_ref, bf16[128,32768]{1,0:T(8,128)(2,1)} %bitcast.11, bf16[128,1024]{1,0:T(8,128)(2,1)S(1)} %collective-permute-done.2.partner_ref), custom_call_target="tpu_custom_call" | custom-call | flops 10000000000 | bytes 30000000 | tf_op jit(solution)/shard_map/sum_step_00/pallas_call | solution.py:271
  18.9 1.6 %give_out.2 = bf16[128,2048]{1,0:T(8,128)(2,1)S(1)} custom-call(s32[51]{0:T(128)S(1)} %get-tuple-element.30.table, bf16[128,32768]{1,0:T(8,128)(2,1)} %bitcast.12, s16[1616,128]{1,0:T(8,128)(2,1)S(1)} %sum_step_00.1._.rest_0_), custom_call_target="tpu_custom_call" | custom-call | flops 1024 | bytes 1024 | tf_op jit(solution)/shard_map/give_out/pallas_call | solution.py:199
  20.6 1.6 %collective-permute-start.3 = (bf16[128,2048]{1,0:T(8,128)(2,1)S(1)}, bf16[128,2048]{1,0:T(8,128)(2,1)S(1)}, u32[]{:S(2)}, u32[]{:S(2)}) collective-permute-start(bf16[128,2048]{1,0:T(8,128)(2,1)S(1)} %give_out.2), channel_id=1, source_target_pairs={{0,4},{4,0},{8,12},{12,8},{16,20},{20,16},{24,28},{28,24},{1,5},{5... | collective-permute-start | bytes 1572872 | tf_op jit(solution)/shard_map/ppermute | solution.py:389
  22.1 2.0 %sum_step_01.1.rest_0_.rest_1_ = s16[1616,128]{1,0:T(8,128)(2,1)S(1)} custom-call(s32[51]{0:T(128)S(1)} %get-tuple-element.30.table, s32[8]{0:T(128)S(1)} %pad_add_fusion.2.counts, s32[2,256]{1,0:T(2,128)S(1)} %pad_add_fusion.pairs_ref, bf16[128,32768]{1,0:T(8,128)(2,1)} %bitcast.13, bf16[128,1024]{1,0:T(8,128)(2,1)S(1)} %collective-permute-done.4.partner_ref, ...), custom_call_target="tpu_custom_call" | custom-call | flops 10000000000 | bytes 30000000 | tf_op jit(solution)/shard_map/sum_step_01/pallas_call | solution.py:271
  24.1 2.0 %collective-permute-start.7 = (s16[1616,128]{1,0:T(8,128)(2,1)S(1)}, s16[1616,128]{1,0:T(8,128)(2,1)S(1)}, u32[]{:S(2)}, u32[]{:S(2)}) collective-permute-start(s16[1616,128]{1,0:T(8,128)(2,1)S(1)} %sum_step_01.1.rest_0_.rest_1_), channel_id=1, source_target_pairs={{0,8},{4,12},{8,0},{12,4},{16,24},{20,28},{24,16},{28,20},{1,9},{5... | collective-permute-start | bytes 1241096 | tf_op jit(solution)/shard_map/ppermute | solution.py:428
  26.2 7.6 %invert_classes_0.1.rest_3_.inverse_ref = f32[2,256,256]{2,1,0:T(8,128)S(1)} custom-call(s32[2]{0:T(128)S(1)} %fusion.counts_ref, s32[2,1024]{1,0:T(2,128)S(1)} %copy-done.1, s16[1616,128]{1,0:T(8,128)(2,1)S(1)} %sum_step_01.1.rest_0_.rest_1_), custom_call_target="tpu_custom_call" | custom-call | flops 1024 | bytes 1024 | tf_op jit(solution)/shard_map/invert_classes_0/pallas_call | solution.py:103
  33.7 2.2 %sum_step_02.1 = (s16[1616,128]{1,0:T(8,128)(2,1)S(1)}, bf16[128,2048]{1,0:T(8,128)(2,1)S(1)}) custom-call(s32[51]{0:T(128)S(1)} %get-tuple-element.30.table, s32[8]{0:T(128)S(1)} %pad_add_fusion.2.counts, s32[2,256]{1,0:T(2,128)S(1)} %pad_add_fusion.pairs_ref, bf16[128,32768]{1,0:T(8,128)(2,1)} %bitcast.14, ...), custom_call_target="tpu_custom_call" | custom-call | flops 10000000000 | bytes 30000000 | tf_op jit(solution)/shard_map/sum_step_02/pallas_call | solution.py:271
  35.9 1.1 collective-permute-start.8
  37.5 0.8 collective-permute-done.7.rest_2_.rest_1_.rest_0_
  38.4 2.2 %sum_step_03.1 = (s16[1616,128]{1,0:T(8,128)(2,1)S(1)}, bf16[128,2048]{1,0:T(8,128)(2,1)S(1)}) custom-call(s32[51]{0:T(128)S(1)} %get-tuple-element.30.table, s32[8]{0:T(128)S(1)} %pad_add_fusion.2.counts, s32[2,256]{1,0:T(2,128)S(1)} %pad_add_fusion.pairs_ref, bf16[128,32768]{1,0:T(8,128)(2,1)} %bitcast.16, ...), custom_call_target="tpu_custom_call" | custom-call | flops 10000000000 | bytes 30000000 | tf_op jit(solution)/shard_map/sum_step_03/pallas_call | solution.py:271
  40.9 2.6 %collective-permute-start.10 = (bf16[128,2048]{1,0:T(8,128)(2,1)S(1)}, bf16[128,2048]{1,0:T(8,128)(2,1)S(1)}, u32[]{:S(2)}, u32[]{:S(2)}) collective-permute-start(bf16[128,2048]{1,0:T(8,128)(2,1)S(1)} %get-tuple-element.20), channel_id=1, source_target_pairs={{0,4},{4,0},{8,12},{12,8},{16,20},{20,16},{24,28},{28,24},{1,5},{5... | collective-permute-start | bytes 1572872 | tf_op jit(solution)/shard_map/ppermute | solution.py:389
  43.6 4.9 %collective-permute-done.8.rest_2_.rest_0_.rest_1_ = s16[1616,128]{1,0:T(8,128)(2,1)S(1)} collective-permute-done((s16[1616,128]{1,0:T(8,128)(2,1)S(1)}, s16[1616,128]{1,0:T(8,128)(2,1)S(1)}, u32[]{:S(2)}, u32[]{:S(2)}) %collective-permute-start.8) | collective-permute-done | bytes 413728 | tf_op jit(solution)/shard_map/ppermute | solution.py:428
  48.5 3.4 %collective-permute-done.6.partner_ref = bf16[128,2048]{1,0:T(8,128)(2,1)S(1)} collective-permute-done((bf16[128,2048]{1,0:T(8,128)(2,1)S(1)}, bf16[128,2048]{1,0:T(8,128)(2,1)S(1)}, u32[]{:S(2)}, u32[]{:S(2)}) %collective-permute-start.6) | collective-permute-done | bytes 524320 | tf_op jit(solution)/shard_map/ppermute | solution.py:389
  51.8 2.0 %sum_step_04.1.rest_2_ = s16[1616,128]{1,0:T(8,128)(2,1)S(1)} custom-call(s32[51]{0:T(128)S(1)} %get-tuple-element.30.table, s32[8]{0:T(128)S(1)} %pad_add_fusion.2.counts, s32[2,256]{1,0:T(2,128)S(1)} %pad_add_fusion.pairs_ref, bf16[128,32768]{1,0:T(8,128)(2,1)} %bitcast.18, bf16[128,2048]{1,0:T(8,128)(2,1)S(1)} %collective-permute-done.6.partner_ref, ...), custom_call_target="tpu_custom_call" | custom-call | flops 10000000000 | bytes 30000000 | tf_op jit(solution)/shard_map/sum_step_04/pallas_call | solution.py:271
  54.5 4.2 %collective-permute-start.13 = (s16[1616,128]{1,0:T(8,128)(2,1)S(1)}, s16[1616,128]{1,0:T(8,128)(2,1)S(1)}, u32[]{:S(2)}, u32[]{:S(2)}) collective-permute-start(s16[1616,128]{1,0:T(8,128)(2,1)S(1)} %sum_step_04.1.rest_2_), channel_id=1, source_target_pairs={{0,8},{4,12},{24,16},{28,20},{1,9},{5,13},{25,17},{29,21},{2,10},{... | collective-permute-start | bytes 1241096 | tf_op jit(solution)/shard_map/ppermute | solution.py:428
  58.7 0.9 collective-permute-done.10.rest_4_.partner_ref
  59.7 2.4 %sum_step_05.1 = (s16[1616,128]{1,0:T(8,128)(2,1)S(1)}, bf16[128,4096]{1,0:T(8,128)(2,1)S(1)}) custom-call(s32[51]{0:T(128)S(1)} %get-tuple-element.30.table, s32[8]{0:T(128)S(1)} %pad_add_fusion.2.counts, s32[2,256]{1,0:T(2,128)S(1)} %pad_add_fusion.pairs_ref, bf16[128,32768]{1,0:T(8,128)(2,1)} %bitcast.20, ...), custom_call_target="tpu_custom_call" | custom-call | flops 10000000000 | bytes 30000000 | tf_op jit(solution)/shard_map/sum_step_05/pallas_call | solution.py:271
  62.8 3.6 %collective-permute-start.12 = (s16[1616,128]{1,0:T(8,128)(2,1)S(1)}, s16[1616,128]{1,0:T(8,128)(2,1)S(1)}, u32[]{:S(2)}, u32[]{:S(2)}) collective-permute-start(s16[1616,128]{1,0:T(8,128)(2,1)S(1)} %get-tuple-element.22.rest_1_), channel_id=1, source_target_pairs={{0,8},{4,12},{24,16},{28,20},{1,9},{5,13},{25,17},{29,21},{2,10},{... | collective-permute-start | bytes 1241096 | tf_op jit(solution)/shard_map/ppermute | solution.py:428
  66.4 0.9 collective-permute-start.11
  67.3 2.0 %sum_step_06.1.rest_1_ = s16[1616,128]{1,0:T(8,128)(2,1)S(1)} custom-call(s32[51]{0:T(128)S(1)} %get-tuple-element.30.table, s32[8]{0:T(128)S(1)} %pad_add_fusion.2.counts, s32[2,256]{1,0:T(2,128)S(1)} %pad_add_fusion.pairs_ref, bf16[128,32768]{1,0:T(8,128)(2,1)} %bitcast.21, bf16[128,2048]{1,0:T(8,128)(2,1)S(1)} %collective-permute-done.10.rest_4_.partner_ref, ...), custom_call_target="tpu_custom_call" | custom-call | flops 10000000000 | bytes 30000000 | tf_op jit(solution)/shard_map/sum_step_06/pallas_call | solution.py:271
  70.1 6.5 %collective-permute-start.16 = (s16[1616,128]{1,0:T(8,128)(2,1)S(1)}, s16[1616,128]{1,0:T(8,128)(2,1)S(1)}, u32[]{:S(2)}, u32[]{:S(2)}) collective-permute-start(s16[1616,128]{1,0:T(8,128)(2,1)S(1)} %sum_step_06.1.rest_1_), channel_id=1, source_target_pairs={{0,8},{4,12},{24,16},{28,20},{1,9},{5,13},{25,17},{29,21},{2,10},{... | collective-permute-start | bytes 1241096 | tf_op jit(solution)/shard_map/ppermute | solution.py:428
  76.6 2.0 %sum_step_07.1.rest_2_ = s16[1616,128]{1,0:T(8,128)(2,1)S(1)} custom-call(s32[51]{0:T(128)S(1)} %get-tuple-element.30.table, s32[8]{0:T(128)S(1)} %pad_add_fusion.2.counts, s32[2,256]{1,0:T(2,128)S(1)} %pad_add_fusion.pairs_ref, bf16[128,32768]{1,0:T(8,128)(2,1)} %bitcast.22, bf16[128,2048]{1,0:T(8,128)(2,1)S(1)} %collective-permute-done.10.rest_4_.partner_ref, ...), custom_call_target="tpu_custom_call" | custom-call | flops 10000000000 | bytes 30000000 | tf_op jit(solution)/shard_map/sum_step_07/pallas_call | solution.py:271
  79.3 7.3 %collective-permute-start.18 = (s16[1616,128]{1,0:T(8,128)(2,1)S(1)}, s16[1616,128]{1,0:T(8,128)(2,1)S(1)}, u32[]{:S(2)}, u32[]{:S(2)}) collective-permute-start(s16[1616,128]{1,0:T(8,128)(2,1)S(1)} %sum_step_07.1.rest_2_), channel_id=1, source_target_pairs={{0,8},{4,12},{24,16},{28,20},{1,9},{5,13},{25,17},{29,21},{2,10},{... | collective-permute-start | bytes 1241096 | tf_op jit(solution)/shard_map/ppermute | solution.py:428
  86.7 0.8 collective-permute-done.11.partner_ref
  87.5 2.2 %sum_step_08.1 = (s16[1616,128]{1,0:T(8,128)(2,1)S(1)}, bf16[128,2048]{1,0:T(8,128)(2,1)S(1)}) custom-call(s32[51]{0:T(128)S(1)} %get-tuple-element.30.table, s32[8]{0:T(128)S(1)} %pad_add_fusion.2.counts, s32[2,256]{1,0:T(2,128)S(1)} %pad_add_fusion.pairs_ref, bf16[128,32768]{1,0:T(8,128)(2,1)} %bitcast.23, ...), custom_call_target="tpu_custom_call" | custom-call | flops 10000000000 | bytes 30000000 | tf_op jit(solution)/shard_map/sum_step_08/pallas_call | solution.py:271
  89.8 1.0 collective-permute-start.22
  90.8 5.8 %collective-permute-done.18.rest_3_.rest_0_ = s16[1616,128]{1,0:T(8,128)(2,1)S(1)} collective-permute-done((s16[1616,128]{1,0:T(8,128)(2,1)S(1)}, s16[1616,128]{1,0:T(8,128)(2,1)S(1)}, u32[]{:S(2)}, u32[]{:S(2)}) %collective-permute-start.18) | collective-permute-done | bytes 413728 | tf_op jit(solution)/shard_map/ppermute | solution.py:428
  96.6 2.2 %sum_step_09.1 = (s16[1616,128]{1,0:T(8,128)(2,1)S(1)}, bf16[128,2048]{1,0:T(8,128)(2,1)S(1)}) custom-call(s32[51]{0:T(128)S(1)} %get-tuple-element.30.table, s32[8]{0:T(128)S(1)} %pad_add_fusion.2.counts, s32[2,256]{1,0:T(2,128)S(1)} %pad_add_fusion.pairs_ref, bf16[128,32768]{1,0:T(8,128)(2,1)} %bitcast.25, ...), custom_call_target="tpu_custom_call" | custom-call | flops 10000000000 | bytes 30000000 | tf_op jit(solution)/shard_map/sum_step_09/pallas_call | solution.py:271
  98.8 2.5 %collective-permute-start.23 = (s16[1616,128]{1,0:T(8,128)(2,1)S(1)}, s16[1616,128]{1,0:T(8,128)(2,1)S(1)}, u32[]{:S(2)}, u32[]{:S(2)}) collective-permute-start(s16[1616,128]{1,0:T(8,128)(2,1)S(1)} %get-tuple-element.25.rest_1_), channel_id=1, source_target_pairs={{0,8},{4,12},{8,24},{12,28},{16,0},{20,4},{24,16},{28,20},{1,9},{5... | collective-permute-start | bytes 1241096 | tf_op jit(solution)/shard_map/ppermute | solution.py:428
  101.4 0.9 collective-permute-start.20
  102.3 3.2 %collective-permute-done.21.rest_2_.rest_4_.rest_5_ = s16[1616,128]{1,0:T(8,128)(2,1)S(1)} collective-permute-done((s16[1616,128]{1,0:T(8,128)(2,1)S(1)}, s16[1616,128]{1,0:T(8,128)(2,1)S(1)}, u32[]{:S(2)}, u32[]{:S(2)}) %collective-permute-start.21) | collective-permute-done | bytes 413728 | tf_op jit(solution)/shard_map/ppermute | solution.py:428
  105.5 2.0 %sum_step_10.1.rest_1_ = s16[1616,128]{1,0:T(8,128)(2,1)S(1)} custom-call(s32[51]{0:T(128)S(1)} %get-tuple-element.30.table, s32[8]{0:T(128)S(1)} %pad_add_fusion.2.counts, s32[2,256]{1,0:T(2,128)S(1)} %pad_add_fusion.pairs_ref, bf16[128,32768]{1,0:T(8,128)(2,1)} %bitcast.27, bf16[128,4096]{1,0:T(8,128)(2,1)S(1)} %collective-permute-done.11.partner_ref, ...), custom_call_target="tpu_custom_call" | custom-call | flops 10000000000 | bytes 30000000 | tf_op jit(solution)/shard_map/sum_step_10/pallas_call | solution.py:271
  107.5 2.5 %collective-permute-start.25 = (s16[1616,128]{1,0:T(8,128)(2,1)S(1)}, s16[1616,128]{1,0:T(8,128)(2,1)S(1)}, u32[]{:S(2)}, u32[]{:S(2)}) collective-permute-start(s16[1616,128]{1,0:T(8,128)(2,1)S(1)} %sum_step_10.1.rest_1_), channel_id=1, source_target_pairs={{0,8},{4,12},{8,24},{12,28},{16,0},{20,4},{24,16},{28,20},{1,9},{5... | collective-permute-start | bytes 1241096 | tf_op jit(solution)/shard_map/ppermute | solution.py:428
  110.0 4.3 %collective-permute-done.23.rest_2_.rest_4_.rest_5_ = s16[1616,128]{1,0:T(8,128)(2,1)S(1)} collective-permute-done((s16[1616,128]{1,0:T(8,128)(2,1)S(1)}, s16[1616,128]{1,0:T(8,128)(2,1)S(1)}, u32[]{:S(2)}, u32[]{:S(2)}) %collective-permute-start.23) | collective-permute-done | bytes 413728 | tf_op jit(solution)/shard_map/ppermute | solution.py:428
  114.3 2.0 %sum_step_11.1 = s16[1616,128]{1,0:T(8,128)(2,1)S(1)} custom-call(s32[51]{0:T(128)S(1)} %get-tuple-element.30.table, s32[8]{0:T(128)S(1)} %pad_add_fusion.2.counts, s32[2,256]{1,0:T(2,128)S(1)} %pad_add_fusion.pairs_ref, bf16[128,32768]{1,0:T(8,128)(2,1)} %bitcast.28, bf16[128,4096]{1,0:T(8,128)(2,1)S(1)} %collective-permute-done.11.partner_ref, ...), custom_call_target="tpu_custom_call" | custom-call | flops 10000000000 | bytes 30000000 | tf_op jit(solution)/shard_map/sum_step_11/pallas_call | solution.py:271
  116.4 2.5 %collective-permute-start.24 = (s16[1616,128]{1,0:T(8,128)(2,1)S(1)}, s16[1616,128]{1,0:T(8,128)(2,1)S(1)}, u32[]{:S(2)}, u32[]{:S(2)}) collective-permute-start(s16[1616,128]{1,0:T(8,128)(2,1)S(1)} %sum_step_11.1), channel_id=1, source_target_pairs={{0,8},{4,12},{8,24},{12,28},{16,0},{20,4},{24,16},{28,20},{1,9},{5... | collective-permute-start | bytes 1241096 | tf_op jit(solution)/shard_map/ppermute | solution.py:428
  118.9 3.5 %finish_0.1.rest_6_ = f32[200,4096]{1,0:T(8,128)} custom-call(s32[51]{0:T(128)S(1)} %get-tuple-element.30.table, s32[8]{0:T(128)S(1)} %pad_add_fusion.2.counts, s32[2,256]{1,0:T(2,128)S(1)} %pad_add_fusion.pairs_ref, bf16[128,32768]{1,0:T(8,128)(2,1)} %bitcast.29, bf16[128,2048]{1,0:T(8,128)(2,1)S(1)} %collective-permute-done.22.rest_3_.partner_ref, ...), custom_call_target="tpu_custom_call" | custom-call | flops 1024 | bytes 1024 | tf_op jit(solution)/shard_map/finish_0/pallas_call | solution.py:339
  122.4 3.6 %finish_1.1.rest_6_ = f32[200,4096]{1,0:T(8,128)} custom-call(s32[51]{0:T(128)S(1)} %get-tuple-element.30.table, s32[8]{0:T(128)S(1)} %pad_add_fusion.2.counts, s32[2,256]{1,0:T(2,128)S(1)} %pad_add_fusion.pairs_ref, bf16[128,32768]{1,0:T(8,128)(2,1)} %bitcast.30, ...), custom_call_target="tpu_custom_call", output_to_operand_aliasing={{}: (12, {})} | custom-call | flops 1024 | bytes 1024 | tf_op jit(solution)/shard_map/finish_1/pallas_call | solution.py:339
  126.0 3.6 %finish_2.1.rest_6_ = f32[200,4096]{1,0:T(8,128)} custom-call(s32[51]{0:T(128)S(1)} %get-tuple-element.30.table, s32[8]{0:T(128)S(1)} %pad_add_fusion.2.counts, s32[2,256]{1,0:T(2,128)S(1)} %pad_add_fusion.pairs_ref, bf16[128,32768]{1,0:T(8,128)(2,1)} %bitcast.31, ...), custom_call_target="tpu_custom_call", output_to_operand_aliasing={{}: (12, {})} | custom-call | flops 1024 | bytes 1024 | tf_op jit(solution)/shard_map/finish_2/pallas_call | solution.py:339
  129.6 3.6 %finish_3.1 = f32[200,4096]{1,0:T(8,128)} custom-call(s32[51]{0:T(128)S(1)} %get-tuple-element.30.table, s32[8]{0:T(128)S(1)} %pad_add_fusion.2.counts, s32[2,256]{1,0:T(2,128)S(1)} %pad_add_fusion.pairs_ref, bf16[128,32768]{1,0:T(8,128)(2,1)} %bitcast.32, ...), custom_call_target="tpu_custom_call", output_to_operand_aliasing={{}: (12, {})} | custom-call | flops 1024 | bytes 1024 | tf_op jit(solution)/shard_map/finish_3/pallas_call | solution.py:339
  (37 shorter events, 6.6 us)
Async XLA Ops:
  0.0 0.7 copy-start
  1.6 11.0 %collective-permute-start = (s32[2]{0:T(128)S(1)}, s32[2]{0:T(128)S(1)}, u32[]{:S(2)}, u32[]{:S(2)}) collective-permute-start(s32[2]{0:T(128)S(1)} %fusion.counts_ref), channel_id=1, source_target_pairs={{0,24},{4,28},{8,16},{12,20},{16,8},{20,12},{24,0},{28,4},{1,25},{... | collective-permute-start | bytes 32 | tf_op jit(solution)/shard_map/ppermute | solution.py:394
  7.7 8.6 %collective-permute-start.2 = (bf16[128,1024]{1,0:T(8,128)(2,1)S(1)}, bf16[128,1024]{1,0:T(8,128)(2,1)S(1)}, u32[]{:S(2)}, u32[]{:S(2)}) collective-permute-start(bf16[128,1024]{1,0:T(8,128)(2,1)S(1)} %dynamic-slice_bitcast_fusion), channel_id=1, source_target_pairs={{0,4},{4,0},{8,12},{12,8},{16,20},{20,16},{24,28},{28,24},{1,5},{5... | collective-permute-start | bytes 786440 | tf_op jit(solution)/shard_map/ppermute | solution.py:389
  12.7 3.5 %collective-permute-start.1 = (s32[4]{0:T(128)S(1)}, s32[4]{0:T(128)S(1)}, u32[]{:S(2)}, u32[]{:S(2)}) collective-permute-start(s32[4]{0:T(128)S(1)} %pad_add_fusion.1), channel_id=1, source_target_pairs={{0,8},{4,12},{8,0},{12,4},{16,24},{20,28},{24,16},{28,20},{1,9},{5... | collective-permute-start | bytes 56 | tf_op jit(solution)/shard_map/ppermute | solution.py:400
  14.2 7.9 %collective-permute-start.4 = (bf16[128,1024]{1,0:T(8,128)(2,1)S(1)}, bf16[128,1024]{1,0:T(8,128)(2,1)S(1)}, u32[]{:S(2)}, u32[]{:S(2)}) collective-permute-start(bf16[128,1024]{1,0:T(8,128)(2,1)S(1)} %give_out.3), channel_id=1, source_target_pairs={{0,4},{4,0},{8,12},{12,8},{16,20},{20,16},{24,28},{28,24},{1,5},{5... | collective-permute-start | bytes 786440 | tf_op jit(solution)/shard_map/ppermute | solution.py:389
  18.3 15.4 %collective-permute-start.5 = (s16[1616,128]{1,0:T(8,128)(2,1)S(1)}, s16[1616,128]{1,0:T(8,128)(2,1)S(1)}, u32[]{:S(2)}, u32[]{:S(2)}) collective-permute-start(s16[1616,128]{1,0:T(8,128)(2,1)S(1)} %sum_step_00.1._.rest_0_), channel_id=1, source_target_pairs={{0,8},{4,12},{8,0},{12,4},{16,24},{20,28},{24,16},{28,20},{1,9},{5... | collective-permute-start | bytes 1241096 | tf_op jit(solution)/shard_map/ppermute | solution.py:428
  20.6 5.6 %copy-start.1 = (s32[2,1024]{1,0:T(2,128)S(1)}, s32[2,1024]{1,0:T(2,128)}, u32[]{:S(2)}) copy-start(s32[2,1024]{1,0:T(2,128)} %pairs_ref.1) | copy-start | bytes 24580
  20.6 13.1 %collective-permute-start.3 = (bf16[128,2048]{1,0:T(8,128)(2,1)S(1)}, bf16[128,2048]{1,0:T(8,128)(2,1)S(1)}, u32[]{:S(2)}, u32[]{:S(2)}) collective-permute-start(bf16[128,2048]{1,0:T(8,128)(2,1)S(1)} %give_out.2), channel_id=1, source_target_pairs={{0,4},{4,0},{8,12},{12,8},{16,20},{20,16},{24,28},{28,24},{1,5},{5... | collective-permute-start | bytes 1572872 | tf_op jit(solution)/shard_map/ppermute | solution.py:389
  24.1 14.3 %collective-permute-start.7 = (s16[1616,128]{1,0:T(8,128)(2,1)S(1)}, s16[1616,128]{1,0:T(8,128)(2,1)S(1)}, u32[]{:S(2)}, u32[]{:S(2)}) collective-permute-start(s16[1616,128]{1,0:T(8,128)(2,1)S(1)} %sum_step_01.1.rest_0_.rest_1_), channel_id=1, source_target_pairs={{0,8},{4,12},{8,0},{12,4},{16,24},{20,28},{24,16},{28,20},{1,9},{5... | collective-permute-start | bytes 1241096 | tf_op jit(solution)/shard_map/ppermute | solution.py:428
  35.9 12.6 %collective-permute-start.8 = (s16[1616,128]{1,0:T(8,128)(2,1)S(1)}, s16[1616,128]{1,0:T(8,128)(2,1)S(1)}, u32[]{:S(2)}, u32[]{:S(2)}) collective-permute-start(s16[1616,128]{1,0:T(8,128)(2,1)S(1)} %get-tuple-element.18.rest_1_), channel_id=1, source_target_pairs={{0,8},{4,12},{8,0},{12,4},{16,24},{20,28},{24,16},{28,20},{1,9},{5... | collective-permute-start | bytes 1241096 | tf_op jit(solution)/shard_map/ppermute | solution.py:428
  37.0 14.9 %collective-permute-start.6 = (bf16[128,2048]{1,0:T(8,128)(2,1)S(1)}, bf16[128,2048]{1,0:T(8,128)(2,1)S(1)}, u32[]{:S(2)}, u32[]{:S(2)}) collective-permute-start(bf16[128,2048]{1,0:T(8,128)(2,1)S(1)} %get-tuple-element.17), channel_id=1, source_target_pairs={{0,4},{4,0},{8,12},{12,8},{16,20},{20,16},{24,28},{28,24},{1,5},{5... | collective-permute-start | bytes 1572872 | tf_op jit(solution)/shard_map/ppermute | solution.py:389
  40.5 18.2 %collective-permute-start.9 = (s16[1616,128]{1,0:T(8,128)(2,1)S(1)}, s16[1616,128]{1,0:T(8,128)(2,1)S(1)}, u32[]{:S(2)}, u32[]{:S(2)}) collective-permute-start(s16[1616,128]{1,0:T(8,128)(2,1)S(1)} %get-tuple-element.19.rest_1_), channel_id=1, source_target_pairs={{0,8},{4,12},{8,0},{12,4},{16,24},{20,28},{24,16},{28,20},{1,9},{5... | collective-permute-start | bytes 1241096 | tf_op jit(solution)/shard_map/ppermute | solution.py:428
  40.9 18.8 %collective-permute-start.10 = (bf16[128,2048]{1,0:T(8,128)(2,1)S(1)}, bf16[128,2048]{1,0:T(8,128)(2,1)S(1)}, u32[]{:S(2)}, u32[]{:S(2)}) collective-permute-start(bf16[128,2048]{1,0:T(8,128)(2,1)S(1)} %get-tuple-element.20), channel_id=1, source_target_pairs={{0,4},{4,0},{8,12},{12,8},{16,20},{20,16},{24,28},{28,24},{1,5},{5... | collective-permute-start | bytes 1572872 | tf_op jit(solution)/shard_map/ppermute | solution.py:389
  53.8 13.5 %collective-permute-start.14 = (s16[1616,128]{1,0:T(8,128)(2,1)S(1)}, s16[1616,128]{1,0:T(8,128)(2,1)S(1)}, u32[]{:S(2)}, u32[]{:S(2)}) collective-permute-start(s16[1616,128]{1,0:T(8,128)(2,1)S(1)} %sum_step_04.1.rest_2_), channel_id=1, source_target_pairs={{8,16},{12,20},{16,8},{20,12},{9,17},{13,21},{17,9},{21,13},{10,18... | collective-permute-start | bytes 1241096 | tf_op jit(solution)/shard_map/ppermute | solution.py:428
  54.5 12.8 %collective-permute-start.13 = (s16[1616,128]{1,0:T(8,128)(2,1)S(1)}, s16[1616,128]{1,0:T(8,128)(2,1)S(1)}, u32[]{:S(2)}, u32[]{:S(2)}) collective-permute-start(s16[1616,128]{1,0:T(8,128)(2,1)S(1)} %sum_step_04.1.rest_2_), channel_id=1, source_target_pairs={{0,8},{4,12},{24,16},{28,20},{1,9},{5,13},{25,17},{29,21},{2,10},{... | collective-permute-start | bytes 1241096 | tf_op jit(solution)/shard_map/ppermute | solution.py:428
  62.1 14.5 %collective-permute-start.15 = (s16[1616,128]{1,0:T(8,128)(2,1)S(1)}, s16[1616,128]{1,0:T(8,128)(2,1)S(1)}, u32[]{:S(2)}, u32[]{:S(2)}) collective-permute-start(s16[1616,128]{1,0:T(8,128)(2,1)S(1)} %get-tuple-element.22.rest_1_), channel_id=1, source_target_pairs={{8,16},{12,20},{16,8},{20,12},{9,17},{13,21},{17,9},{21,13},{10,18... | collective-permute-start | bytes 1241096 | tf_op jit(solution)/shard_map/ppermute | solution.py:428
  62.8 13.8 %collective-permute-start.12 = (s16[1616,128]{1,0:T(8,128)(2,1)S(1)}, s16[1616,128]{1,0:T(8,128)(2,1)S(1)}, u32[]{:S(2)}, u32[]{:S(2)}) collective-permute-start(s16[1616,128]{1,0:T(8,128)(2,1)S(1)} %get-tuple-element.22.rest_1_), channel_id=1, source_target_pairs={{0,8},{4,12},{24,16},{28,20},{1,9},{5,13},{25,17},{29,21},{2,10},{... | collective-permute-start | bytes 1241096 | tf_op jit(solution)/shard_map/ppermute | solution.py:428
  66.4 21.0 %collective-permute-start.11 = (bf16[128,4096]{1,0:T(8,128)(2,1)S(1)}, bf16[128,4096]{1,0:T(8,128)(2,1)S(1)}, u32[]{:S(2)}, u32[]{:S(2)}) collective-permute-start(bf16[128,4096]{1,0:T(8,128)(2,1)S(1)} %get-tuple-element.21), channel_id=1, source_target_pairs={{0,4},{4,0},{8,12},{12,8},{16,20},{20,16},{24,28},{28,24},{1,5},{5... | collective-permute-start | bytes 3145736 | tf_op jit(solution)/shard_map/ppermute | solution.py:389
  69.4 17.3 %collective-permute-start.17 = (s16[1616,128]{1,0:T(8,128)(2,1)S(1)}, s16[1616,128]{1,0:T(8,128)(2,1)S(1)}, u32[]{:S(2)}, u32[]{:S(2)}) collective-permute-start(s16[1616,128]{1,0:T(8,128)(2,1)S(1)} %sum_step_06.1.rest_1_), channel_id=1, source_target_pairs={{8,16},{12,20},{16,8},{20,12},{9,17},{13,21},{17,9},{21,13},{10,18... | collective-permute-start | bytes 1241096 | tf_op jit(solution)/shard_map/ppermute | solution.py:428
  70.1 16.6 %collective-permute-start.16 = (s16[1616,128]{1,0:T(8,128)(2,1)S(1)}, s16[1616,128]{1,0:T(8,128)(2,1)S(1)}, u32[]{:S(2)}, u32[]{:S(2)}) collective-permute-start(s16[1616,128]{1,0:T(8,128)(2,1)S(1)} %sum_step_06.1.rest_1_), channel_id=1, source_target_pairs={{0,8},{4,12},{24,16},{28,20},{1,9},{5,13},{25,17},{29,21},{2,10},{... | collective-permute-start | bytes 1241096 | tf_op jit(solution)/shard_map/ppermute | solution.py:428
  78.6 12.2 %collective-permute-start.19 = (s16[1616,128]{1,0:T(8,128)(2,1)S(1)}, s16[1616,128]{1,0:T(8,128)(2,1)S(1)}, u32[]{:S(2)}, u32[]{:S(2)}) collective-permute-start(s16[1616,128]{1,0:T(8,128)(2,1)S(1)} %sum_step_07.1.rest_2_), channel_id=1, source_target_pairs={{8,16},{12,20},{16,8},{20,12},{9,17},{13,21},{17,9},{21,13},{10,18... | collective-permute-start | bytes 1241096 | tf_op jit(solution)/shard_map/ppermute | solution.py:428
  79.3 17.3 %collective-permute-start.18 = (s16[1616,128]{1,0:T(8,128)(2,1)S(1)}, s16[1616,128]{1,0:T(8,128)(2,1)S(1)}, u32[]{:S(2)}, u32[]{:S(2)}) collective-permute-start(s16[1616,128]{1,0:T(8,128)(2,1)S(1)} %sum_step_07.1.rest_2_), channel_id=1, source_target_pairs={{0,8},{4,12},{24,16},{28,20},{1,9},{5,13},{25,17},{29,21},{2,10},{... | collective-permute-start | bytes 1241096 | tf_op jit(solution)/shard_map/ppermute | solution.py:428
  89.7 15.8 %collective-permute-start.21 = (s16[1616,128]{1,0:T(8,128)(2,1)S(1)}, s16[1616,128]{1,0:T(8,128)(2,1)S(1)}, u32[]{:S(2)}, u32[]{:S(2)}) collective-permute-start(s16[1616,128]{1,0:T(8,128)(2,1)S(1)} %get-tuple-element.23.rest_2_), channel_id=1, source_target_pairs={{0,8},{4,12},{8,24},{12,28},{16,0},{20,4},{24,16},{28,20},{1,9},{5... | collective-permute-start | bytes 1241096 | tf_op jit(solution)/shard_map/ppermute | solution.py:428
  89.8 15.7 %collective-permute-start.22 = (bf16[128,2048]{1,0:T(8,128)(2,1)S(1)}, bf16[128,2048]{1,0:T(8,128)(2,1)S(1)}, u32[]{:S(2)}, u32[]{:S(2)}) collective-permute-start(bf16[128,2048]{1,0:T(8,128)(2,1)S(1)} %get-tuple-element.26), channel_id=1, source_target_pairs={{0,4},{4,0},{8,12},{12,8},{16,20},{20,16},{24,28},{28,24},{1,5},{5... | collective-permute-start | bytes 1572872 | tf_op jit(solution)/shard_map/ppermute | solution.py:389
  98.8 15.5 %collective-permute-start.23 = (s16[1616,128]{1,0:T(8,128)(2,1)S(1)}, s16[1616,128]{1,0:T(8,128)(2,1)S(1)}, u32[]{:S(2)}, u32[]{:S(2)}) collective-permute-start(s16[1616,128]{1,0:T(8,128)(2,1)S(1)} %get-tuple-element.25.rest_1_), channel_id=1, source_target_pairs={{0,8},{4,12},{8,24},{12,28},{16,0},{20,4},{24,16},{28,20},{1,9},{5... | collective-permute-start | bytes 1241096 | tf_op jit(solution)/shard_map/ppermute | solution.py:428
  101.4 24.6 %collective-permute-start.20 = (bf16[128,2048]{1,0:T(8,128)(2,1)S(1)}, bf16[128,2048]{1,0:T(8,128)(2,1)S(1)}, u32[]{:S(2)}, u32[]{:S(2)}) collective-permute-start(bf16[128,2048]{1,0:T(8,128)(2,1)S(1)} %get-tuple-element.24), channel_id=1, source_target_pairs={{0,4},{4,0},{8,12},{12,8},{16,20},{20,16},{24,28},{28,24},{1,5},{5... | collective-permute-start | bytes 1572872 | tf_op jit(solution)/shard_map/ppermute | solution.py:389
  107.5 18.5 %collective-permute-start.25 = (s16[1616,128]{1,0:T(8,128)(2,1)S(1)}, s16[1616,128]{1,0:T(8,128)(2,1)S(1)}, u32[]{:S(2)}, u32[]{:S(2)}) collective-permute-start(s16[1616,128]{1,0:T(8,128)(2,1)S(1)} %sum_step_10.1.rest_1_), channel_id=1, source_target_pairs={{0,8},{4,12},{8,24},{12,28},{16,0},{20,4},{24,16},{28,20},{1,9},{5... | collective-permute-start | bytes 1241096 | tf_op jit(solution)/shard_map/ppermute | solution.py:428
  116.4 13.2 %collective-permute-start.24 = (s16[1616,128]{1,0:T(8,128)(2,1)S(1)}, s16[1616,128]{1,0:T(8,128)(2,1)S(1)}, u32[]{:S(2)}, u32[]{:S(2)}) collective-permute-start(s16[1616,128]{1,0:T(8,128)(2,1)S(1)} %sum_step_11.1), channel_id=1, source_target_pairs={{0,8},{4,12},{8,24},{12,28},{16,0},{20,4},{24,16},{28,20},{1,9},{5... | collective-permute-start | bytes 1241096 | tf_op jit(solution)/shard_map/ppermute | solution.py:428
